TPU v7x, 32 devices: a whole 2x2x4 slice. The times are simulated.
32 devices in a mesh: gx: 4 (over x, core), gy: 2 (over y), gz: 4 (over z).
Axes of the slice: x: 2, y: 2, z: 4, core: 2. Of those that a mesh axis runs over, the one named last changes fastest.
Arguments:
- right_side: float32 [32, 16, 512], P('gx', 'gy', 'gz'), may hold values from -8 to 8
- geometry: float32 [4, 32, 16, 512], P(None, 'gx', 'gy', 'gz'), may hold values from 0.02 to 0.2
- element_shape_class: int32 [4, 2, 64], P('gx', 'gy', 'gz'), may hold values from 0 to 31
- fdm_vectors: float32 [32, 3, 10, 10], replicated, may hold values from -1 to 2
- fdm_values: float32 [32, 3, 10], replicated, may hold values from 0.3 to 10
Outputs:
- solution: float32 [32, 16, 512], P('gx', 'gy', 'gz')
- residual: float32 [32, 16, 512], P('gx', 'gy', 'gz')
All inputs are finite; a program needn't handle non-finite values.
Results may differ from a plain program's by a relative error of at most 0.0003.
Values sent between devices are 32-bit elements; how exact they have to be, the bound alone decides.
A program may use at most 64 MiB of HBM per device.

v0:
```python
import jax
import jax.numpy as jnp
import numpy as np
from jax import lax
from jax.experimental import pallas as pl
from jax.experimental.pallas import tpu as pltpu
from jax.sharding import PartitionSpec as P

HIGHEST = lax.Precision.HIGHEST
MESH = pl.DeviceIdType.MESH
F32 = jnp.float32
BF16 = jnp.bfloat16
DIRECTIONS = ((1, 0), (-1, 0), (0, 1), (0, -1), (1, 1), (1, -1), (-1, 1), (-1, -1))
STARTS = (0, 16, 32, 48, 64, 72, 80, 88, 96)
ROUNDS = 5


def derivative_table():
    points = np.array(
        [
            -1.0,
            -0.8717401485096066,
            -0.5917001814331423,
            -0.2092992179024789,
            0.2092992179024789,
            0.5917001814331423,
            0.8717401485096066,
            1.0,
        ]
    )
    previous = np.ones(8)
    current = points * 1.0
    for order in range(1, 7):
        following = ((2 * order + 1) * points * current - order * previous) / (order + 1)
        previous = current
        current = following
    spacing = points[:, None] - points[None, :] + np.eye(8)
    off_diagonal = current[:, None] / (current[None, :] * spacing)
    positions = np.arange(8)
    end_values = np.where(positions == 0, -14.0, 0.0) + np.where(positions == 7, 14.0, 0.0)
    return np.where(np.eye(8) > 0, np.eye(8) * end_values[None, :], off_diagonal)


def message_rows(sent):
    own = tuple(range(1, 9))
    for place, (dx, dy) in enumerate(DIRECTIONS):
        xs = sent[dx] if dx else own
        ys = sent[dy] if dy else own
        if dy and not dx:
            pairs = [(x, y) for y in ys for x in xs]
        else:
            pairs = [(x, y) for x in xs for y in ys]
        for number, (x, y) in enumerate(pairs):
            yield STARTS[place] + number, x, y


def node_row(x, y):
    return (x - 1) * 8 + y - 1


def slot_row(x, y):
    return x * 16 + y


def selections():
    gather_from = {1: (7, 8), -1: (2, 1)}
    gather_to = {1: (0, 1), -1: (9, 8)}
    scatter_from = {1: (9, 8), -1: (0, 1)}
    scatter_to = {1: (2, 1), -1: (7, 8)}
    pack_gather = np.zeros((96, 64))
    unpack_gather = np.zeros((160, 160))
    pack_scatter = np.zeros((96, 160))
    unpack_scatter = np.zeros((64, 256))
    for x in range(1, 9):
        for y in range(1, 9):
            unpack_gather[slot_row(x, y), node_row(x, y)] = 1
            unpack_scatter[node_row(x, y), slot_row(x, y)] = 1
    for row, x, y in message_rows(gather_from):
        pack_gather[row, node_row(x, y)] = 1
    for row, x, y in message_rows(gather_to):
        unpack_gather[slot_row(x, y), 64 + row] = 1
    for row, x, y in message_rows(scatter_from):
        pack_scatter[row, slot_row(x, y)] = 1
    for row, x, y in message_rows(scatter_to):
        unpack_scatter[node_row(x, y), 160 + row] = 1
    depth = np.zeros((64, 256))
    for row, lane in enumerate((126, 127, 1, 0)):
        depth[row, lane] = 1
    for row, lane in ((0, 128), (1, 0), (10, 129), (11, 127)):
        depth[16 + row, lane] = 1
    for row, lane in enumerate((129, 127, 128, 0)):
        depth[32 + row, lane] = 1
    for row, lane in ((0, 1), (1, 0), (10, 126), (11, 127)):
        depth[48 + row, lane] = 1
    table = np.zeros((480, 256))
    for start, part in (
        (0, pack_gather),
        (96, unpack_gather),
        (256, pack_scatter),
        (352, unpack_scatter),
        (416, depth),
    ):
        table[start : start + part.shape[0], : part.shape[1]] = part
    return table


def derivative_matrices():
    derivative = derivative_table()
    eye = np.eye(8)
    plane = np.concatenate([np.kron(derivative, eye), np.kron(eye, derivative)], 0)
    deep = np.kron(np.eye(16), derivative)
    table = np.zeros((448, 128))
    table[0:128, :64] = plane
    table[128:192] = plane.T
    table[192:320] = deep.T
    table[320:448] = deep
    return table


def pieces(value):
    high = value.astype(BF16)
    rest = value - high.astype(F32)
    middle = rest.astype(BF16)
    low = (rest - middle.astype(F32)).astype(BF16)
    return low, middle, high


def pick(chooser, value, dims):
    total = None
    for piece in pieces(value):
        part = lax.dot_general(chooser, piece, (dims, ((), ())), preferred_element_type=F32)
        total = part if total is None else total + part
    return total


def place(value, chooser, dims):
    total = None
    for piece in pieces(value):
        part = lax.dot_general(piece, chooser, (dims, ((), ())), preferred_element_type=F32)
        total = part if total is None else total + part
    return total


def kernel(
    counts,
    right_ref,
    geometry_ref,
    class_ref,
    table_ref,
    select_ref,
    derive_ref,
    solution_ref,
    residual_ref,
    deep_send,
    deep_recv,
    plane_send,
    plane_recv,
    first_ref,
    second_ref,
    second_back_ref,
    third_ref,
    third_back_ref,
    inverse_ref,
    sums_plane,
    sums_line,
    deep_sems,
    plane_sems,
    sum_send_sems,
    sum_plane_sems,
    line_send_sems,
    sum_line_sems,
):
    nx, ny, nz = counts
    gx, gy, gz = lax.axis_index("gx"), lax.axis_index("gy"), lax.axis_index("gz")
    plane_size = nx * ny
    me_plane = gx * ny + gy

    deep_recv[...] = jnp.zeros_like(deep_recv)
    plane_recv[...] = jnp.zeros_like(plane_recv)
    deep_send[...] = jnp.zeros_like(deep_send)

    def plane_partner(offset):
        other = lax.rem(me_plane + offset, plane_size)
        return other, (other // ny, lax.rem(other, ny), gz)

    def line_partner(offset):
        other = lax.rem(gz + offset, nz)
        return other, (gx, gy, other)

    barrier = pltpu.get_barrier_semaphore()
    for offset in range(1, plane_size):
        pl.semaphore_signal(
            barrier, inc=1, device_id=plane_partner(offset)[1], device_id_type=MESH
        )
    for offset in range(1, nz):
        pl.semaphore_signal(barrier, inc=1, device_id=line_partner(offset)[1], device_id_type=MESH)
    pl.semaphore_wait(barrier, plane_size + nz - 2)

    def deep_copy(number, step):
        side = 0 if step > 0 else 1
        return pltpu.make_async_remote_copy(
            src_ref=deep_send.at[number],
            dst_ref=deep_recv.at[number, pl.ds(8 * side, 8)],
            send_sem=deep_sems.at[0, number, side],
            recv_sem=deep_sems.at[1, number, side],
            device_id=(gx, gy, gz + step),
            device_id_type=MESH,
        )

    def deep_exists(step):
        return gz + 1 < nz if step > 0 else gz > 0

    def deep_start(number, message):
        deep_send[number, :, 0:64] = message
        for step in (1, -1):
            pl.when(deep_exists(step))(lambda step=step: deep_copy(number, step).start())

    def deep_wait(number):
        for step in (1, -1):
            pl.when(deep_exists(-step))(lambda step=step: deep_copy(number, step).wait_recv())
        return deep_recv[number][:, 0:64]

    def plane_copy(number, at):
        dx, dy = DIRECTIONS[at]
        rows = pl.ds(STARTS[at], STARTS[at + 1] - STARTS[at])
        return pltpu.make_async_remote_copy(
            src_ref=plane_send.at[number, rows],
            dst_ref=plane_recv.at[number, rows],
            send_sem=plane_sems.at[0, number, at],
            recv_sem=plane_sems.at[1, number, at],
            device_id=(gx + dx, gy + dy, gz),
            device_id_type=MESH,
        )

    def plane_exists(dx, dy):
        x, y = gx + dx, gy + dy
        return (x >= 0) & (x < nx) & (y >= 0) & (y < ny)

    def plane_start(number, message):
        plane_send[number] = message
        for at, (dx, dy) in enumerate(DIRECTIONS):
            pl.when(plane_exists(dx, dy))(lambda at=at: plane_copy(number, at).start())

    def plane_wait(number):
        for at, (dx, dy) in enumerate(DIRECTIONS):
            pl.when(plane_exists(-dx, -dy))(lambda at=at: plane_copy(number, at).wait_recv())
        return plane_recv[number]

    rows = lax.broadcasted_iota(jnp.int32, (64, 128), 0)
    lanes = lax.broadcasted_iota(jnp.int32, (64, 128), 1)
    rows_rows = ((1,), (1,))
    plain = ((1,), (0,))
    columns = ((0,), (0,))

    def gather_deep_start(number, field):
        deep_start(number, pick(select_ref[416:424, 0:128], field, rows_rows))

    def gather_deep_end(number, field):
        node = lax.rem(lanes, 8)
        following = jnp.where((node == 7) & (lanes < 127), pltpu.roll(field, 127, 1), 0.0)
        previous = jnp.where((node == 0) & (lanes > 0), pltpu.roll(field, 1, 1), 0.0)
        wide = jnp.concatenate([field + following + previous, jnp.zeros_like(field)], 1)
        return wide + place(deep_wait(number), select_ref[432:448, :], columns)

    def gather_plane_start(number, wide):
        plane_start(number, pick(select_ref[0:96, 0:64], wide, plain))

    def gather_plane_end(number, wide):
        both = jnp.concatenate([wide, plane_wait(number)], 0)
        return pick(select_ref[96:256, 0:160], both, plain)

    def scatter(number, extended):
        plane_start(number, pick(select_ref[256:352, 0:160], extended, plain))
        both = jnp.concatenate([extended, plane_wait(number)], 0)
        wide = pick(select_ref[352:416, :], both, plain)
        deep_start(number, pick(select_ref[448:456, :], wide, rows_rows))
        return wide[:, 0:128] + place(deep_wait(number), select_ref[464:480, 0:128], columns)

    def solve(extended):
        value = jnp.dot(extended, third_ref[...], precision=HIGHEST).reshape(10, 16, 256)
        total = first_ref[0] * value[0][None]
        for a in range(1, 10):
            total = total + first_ref[a] * value[a][None]
        value = total
        total = second_ref[0][None] * value[:, 0:1, :]
        for b in range(1, 10):
            total = total + second_ref[b][None] * value[:, b : b + 1, :]
        value = total * inverse_ref[...]
        total = second_back_ref[0][None] * value[:, 0:1, :]
        for n in range(1, 10):
            total = total + second_back_ref[n][None] * value[:, n : n + 1, :]
        value = total
        total = first_ref[:, 0] * value[0][None]
        for m in range(1, 10):
            total = total + first_ref[:, m] * value[m][None]
        return lax.dot_general(
            total.reshape(160, 256), third_back_ref[...], (rows_rows, ((), ())), precision=HIGHEST
        )

    def local(field):
        slopes = jnp.dot(derive_ref[0:128, 0:64], field, precision=HIGHEST)
        deep = jnp.dot(field, derive_ref[192:320, :], precision=HIGHEST)
        back = jnp.dot(derive_ref[128:192, :], geometry_ref[0:128] * slopes, precision=HIGHEST)
        deep = jnp.dot(geometry_ref[128:192] * deep, derive_ref[320:448, :], precision=HIGHEST)
        return back + deep + geometry_ref[192:256] * field

    def factor(inside, length, device, devices):
        last = (device == devices - 1) & (inside == length - 1)
        first = (device == 0) & (inside == 0)
        node = lax.rem(inside, 8)
        shared = ((node == 7) & ~last) | ((node == 0) & ~first)
        return jnp.where(shared, 0.5, 1.0).astype(F32)

    weight = (
        factor(rows // 8, 8, gx, nx) * factor(lax.rem(rows, 8), 8, gy, ny)
        * factor(lanes, 128, gz, nz)
    )
    right = right_ref[...]
    weighted = weight * right
    gather_deep_start(0, weighted)

    classes = class_ref[...]
    chooser = (lax.broadcasted_iota(jnp.int32, (32, 256), 0) == classes).astype(F32).astype(BF16)
    table = place(table_ref[...], chooser, plain)
    for a in range(10):
        for m in range(10):
            first_ref[a, m] = jnp.broadcast_to(table[a * 10 + m : a * 10 + m + 1], (16, 256))
    second_ref[...] = table[104:264].reshape(10, 16, 256)
    second_back_ref[...] = table[264:424].reshape(10, 16, 256)
    mode = lax.broadcasted_iota(jnp.int32, (1, 256), 1) // 16
    third = jnp.zeros((16, 256), F32)
    level = jnp.zeros((1, 256), F32)
    for p in range(10):
        third = third + jnp.where(mode == p, table[424 + 16 * p : 440 + 16 * p], 0.0)
        level = level + jnp.where(mode == p, table[616 + p : 617 + p], 0.0)

    wide = gather_deep_end(0, weighted)
    gather_plane_start(0, wide)

    for m in range(10):
        inverse_ref[m] = 1.0 / (table[600 + m : 601 + m] + table[584:600] + level)
    node = lax.broadcasted_iota(jnp.int32, (256, 256), 0)
    element = lax.rem(lax.broadcasted_iota(jnp.int32, (256, 256), 1), 16)
    reach = jnp.where(node == 128, -2, node) - 8 * element
    slot = jnp.where(
        reach == -2, 0, jnp.where(reach == 9, 9, jnp.where((reach >= 0) & (reach < 8), reach + 1, -1))
    )
    slot_back = jnp.where(reach == 8, 8, jnp.where(reach == -1, 1, slot))
    spread = jnp.zeros((256, 256), F32)
    spread_back = jnp.zeros((256, 256), F32)
    for c in range(10):
        spread = jnp.where(slot == c, third[c : c + 1], spread)
        spread_back = jnp.where(slot_back == c, third[c : c + 1], spread_back)
    third_ref[...] = spread
    third_back_ref[...] = spread_back

    extended = gather_plane_end(0, wide)
    precond = scatter(1, solve(extended))
    image_local = local(precond)
    gather_deep_start(2, image_local)
    wide = gather_deep_end(2, image_local)
    gather_plane_start(2, wide)
    extended = gather_plane_end(2, wide)
    image = jnp.concatenate(
        [extended[16 * x + 1 : 16 * x + 9, 0:128] for x in range(1, 9)], 0
    )
    again = scatter(3, solve(extended))
    again_local = local(again)

    products = (
        weighted * precond,
        precond * image_local,
        weighted * again,
        weight * image * again,
        precond * again_local,
        again * again_local,
    )
    kind = lax.broadcasted_iota(jnp.int32, (8, 128), 0)
    packed = jnp.zeros((8, 128), F32)
    for number, product in enumerate(products):
        packed = packed + jnp.where(kind == number, jnp.sum(product, 0, keepdims=True), 0.0)

    def sum_copy(buffer, send_sems, recv_sems, offset, mine, partner):
        return pltpu.make_async_remote_copy(
            src_ref=buffer.at[mine],
            dst_ref=buffer.at[mine],
            send_sem=send_sems.at[offset - 1],
            recv_sem=recv_sems.at[mine],
            device_id=partner,
            device_id_type=MESH,
        )

    def sum_wait(buffer, recv_sems, other):
        pltpu.make_async_copy(buffer.at[other], buffer.at[other], recv_sems.at[other]).wait()

    sums_plane[me_plane] = packed
    for offset in range(1, plane_size):
        sum_copy(
            sums_plane, sum_send_sems, sum_plane_sems, offset, me_plane, plane_partner(offset)[1]
        ).start()
    gather_deep_start(4, again_local)
    wide = gather_deep_end(4, again_local)
    gather_plane_start(4, wide)
    for offset in range(1, plane_size):
        sum_wait(sums_plane, sum_plane_sems, plane_partner(offset)[0])
    sums_line[gz] = jnp.sum(sums_plane[...], 0)
    for offset in range(1, nz):
        sum_copy(
            sums_line, line_send_sems, sum_line_sems, offset, gz, line_partner(offset)[1]
        ).start()
    extended = gather_plane_end(4, wide)
    again_image = jnp.concatenate(
        [extended[16 * x + 1 : 16 * x + 9, 0:128] for x in range(1, 9)], 0
    )
    for offset in range(1, nz):
        sum_wait(sums_line, sum_line_sems, line_partner(offset)[0])
    sums = jnp.sum(jnp.sum(sums_line[...], 0), 1, keepdims=True)
    a, b, c, d, e, f = [sums[k : k + 1] for k in range(6)]
    step_one = a / b
    rho = a - step_one * (b + c) + step_one * step_one * d
    stretch = 1.0 + rho / a
    curvature = stretch * stretch * b - stretch * step_one * (d + e) + step_one * step_one * f
    step_two = rho / curvature
    on_precond = step_one + step_two * stretch
    on_again = step_one * step_two
    solution_ref[...] = on_precond * precond - on_again * again
    residual_ref[...] = right - on_precond * image + on_again * again_image

    for number in range(ROUNDS):
        for step in (1, -1):
            pl.when(deep_exists(step))(
                lambda number=number, step=step: deep_copy(number, step).wait_send()
            )
        for at, (dx, dy) in enumerate(DIRECTIONS):
            pl.when(plane_exists(dx, dy))(
                lambda number=number, at=at: plane_copy(number, at).wait_send()
            )
    for offset in range(1, plane_size):
        sum_copy(
            sums_plane, sum_send_sems, sum_plane_sems, offset, me_plane, plane_partner(offset)[1]
        ).wait_send()
    for offset in range(1, nz):
        sum_copy(
            sums_line, line_send_sems, sum_line_sems, offset, gz, line_partner(offset)[1]
        ).wait_send()


def on_device(counts, right_side, geometry, element_shape_class, fdm_vectors, fdm_values):
    nx, ny, nz = counts
    shape = right_side.shape
    classes = jnp.tile(element_shape_class.reshape(1, 16), (1, 16))
    turned = jnp.transpose(fdm_vectors, (1, 2, 3, 0))
    levels = jnp.transpose(fdm_values, (1, 2, 0))

    def padded(part):
        return jnp.pad(part, ((0, 0), (0, 6), (0, 0))).reshape(160, 32)

    table = jnp.concatenate(
        [
            turned[0].reshape(100, 32),
            jnp.zeros((4, 32), F32),
            padded(turned[1]),
            padded(jnp.swapaxes(turned[1], 0, 1)),
            padded(jnp.swapaxes(turned[2], 0, 1)),
            jnp.pad(levels[1], ((0, 6), (0, 0))),
            jnp.pad(levels[0], ((0, 6), (0, 0))),
            jnp.pad(levels[2], ((0, 6), (0, 0))),
        ],
        0,
    )
    vmem = pl.BlockSpec(memory_space=pltpu.VMEM)
    solved, left = pl.pallas_call(
        lambda *refs: kernel(counts, *refs),
        out_shape=(jax.ShapeDtypeStruct((64, 128), F32),) * 2,
        in_specs=[vmem] * 6,
        out_specs=(vmem, vmem),
        scratch_shapes=[
            pltpu.VMEM((ROUNDS, 8, 128), F32),
            pltpu.VMEM((ROUNDS, 16, 128), F32),
            pltpu.VMEM((ROUNDS, 96, 256), F32),
            pltpu.VMEM((ROUNDS, 96, 256), F32),
            pltpu.VMEM((10, 10, 16, 256), F32),
            pltpu.VMEM((10, 16, 256), F32),
            pltpu.VMEM((10, 16, 256), F32),
            pltpu.VMEM((256, 256), F32),
            pltpu.VMEM((256, 256), F32),
            pltpu.VMEM((10, 16, 256), F32),
            pltpu.VMEM((nx * ny, 8, 128), F32),
            pltpu.VMEM((nz, 8, 128), F32),
            pltpu.SemaphoreType.DMA((2, ROUNDS, 2)),
            pltpu.SemaphoreType.DMA((2, ROUNDS, 8)),
            pltpu.SemaphoreType.DMA((nx * ny,)),
            pltpu.SemaphoreType.DMA((nx * ny,)),
            pltpu.SemaphoreType.DMA((nz,)),
            pltpu.SemaphoreType.DMA((nz,)),
        ],
        compiler_params=pltpu.CompilerParams(
            collective_id=0, has_side_effects=True, vmem_limit_bytes=32 * 1024 * 1024
        ),
    )(
        right_side.reshape(64, 128),
        geometry.reshape(256, 128),
        classes,
        table,
        jnp.asarray(selections(), BF16),
        jnp.asarray(derivative_matrices(), F32),
    )
    return solved.reshape(shape), left.reshape(shape)


def solution(mesh):
    counts = tuple(mesh.shape[name] for name in ("gx", "gy", "gz"))
    placed = (P("gx", "gy", "gz"), P(None, "gx", "gy", "gz"), P("gx", "gy", "gz"), P(), P())
    return jax.shard_map(
        lambda *arrays: on_device(counts, *arrays),
        mesh=mesh,
        in_specs=placed,
        out_specs=(P("gx", "gy", "gz"), P("gx", "gy", "gz")),
        check_vma=False,
    )
```

profile of v0, /device:TPU:0, one launch (start us, length us, event | category | flops | bytes accessed | tf_op | source)
XLA Modules:
  0.0 47.7 jit_solution(4483269774496010716)
XLA Ops:
  0.6 1.4 %fusion = (f32[1,10,10,32]{3,0,2,1:T(1,128)S(1)}, f32[1,10,10,32]{3,0,2,1:T(1,128)S(1)}, f32[10,10,32]{2,1,0:T(8,128)S(1)}) fusion(f32[3,10,10,32]{3,0,2,1:T(4,128)} %bitcast.38), kind=kLoop, calls=%fused_computation.8 | loop fusion | bytes 76800 | tf_op jit(solution)/shard_map/slice | solution.py:464
  2.2 0.0 copy-start.4
  2.2 0.7 %copy-done.4 = f32[32,3,10]{0,1,2:T(4,128)S(1)} copy-done((f32[32,3,10]{0,1,2:T(4,128)S(1)}, f32[32,3,10]{0,1,2:T(4,128)}, u32[]{:S(2)}) %copy-start.4) | copy-done | bytes 3864
  2.9 0.0 copy-start
  3.0 0.0 copy-start.1
  3.0 0.0 copy-start.2
  3.0 0.0 copy-start.3
  3.0 0.0 copy-start.5
  3.0 0.8 %copy-done.5 = s32[1,1,16]{2,1,0:T(1,128)S(1)} copy-done((s32[1,1,16]{2,1,0:T(1,128)S(1)}, s32[1,1,16]{2,1,0:T(1,128)}, u32[]{:S(2)}) %copy-start.5) | copy-done | bytes 88
  3.8 0.1 tile.12.refs_2_
  3.9 0.0 copy-done
  3.9 0.1 copy-done.1
  4.0 0.1 copy-done.2
  4.1 0.0 copy-done.3
  4.1 42.3 %shard_map.86 = (f32[64,128]{1,0:T(8,128)S(1)}, f32[64,128]{1,0:T(8,128)S(1)}) custom-call(f32[64,128]{1,0:T(8,128)S(1)} %bitcast.31, f32[256,128]{1,0:T(8,128)S(1)} %bitcast.30, s32[1,256]{1,0:T(1,128)S(1)} %tile.12.refs_2_, f32[632,32]{1,0:T(8,128)S(1)} %concatenate.3.refs_3_, bf16[480,256]{1,0:T(8,128)(2,1)S(1)} %copy-done, f32[448,128]{1,0:T(8,128)S(1)} %copy-done.1), custom_call_target="tpu_custom_call" | custom-call | tf_op jit(solution)/shard_map/pallas_call | solution.py:472
  46.5 0.6 %copy.47 = f32[8,8,128]{2,1,0:T(8,128)} copy(f32[8,8,128]{2,1,0:T(8,128)S(1)} %bitcast.33) | data formatting | bytes 65536
  47.1 0.6 %copy.48 = f32[8,8,128]{2,1,0:T(8,128)} copy(f32[8,8,128]{2,1,0:T(8,128)S(1)} %bitcast.32) | data formatting | bytes 65536
  (14 shorter events, 0.1 us)
Async XLA Ops:
  2.2 0.7 %copy-start.4 = (f32[32,3,10]{0,1,2:T(4,128)S(1)}, f32[32,3,10]{0,1,2:T(4,128)}, u32[]{:S(2)}) copy-start(f32[32,3,10]{0,1,2:T(4,128)} %param.11) | copy-start | bytes 11524
  2.9 0.9 %copy-start = (bf16[480,256]{1,0:T(8,128)(2,1)S(1)}, bf16[480,256]{1,0:T(8,128)(2,1)}, u32[]{:S(2)}) copy-start(bf16[480,256]{1,0:T(8,128)(2,1)} %constant.8.clone.refs_4_) | copy-start | bytes 737284
  3.0 1.1 %copy-start.1 = (f32[448,128]{1,0:T(8,128)S(1)}, f32[448,128]{1,0:T(8,128)}, u32[]{:S(2)}) copy-start(f32[448,128]{1,0:T(8,128)} %constant.9.clone.refs_5_) | copy-start | bytes 688132
  3.0 1.1 %copy-start.2 = (f32[4,8,8,128]{3,2,1,0:T(8,128)S(1)}, f32[4,8,8,128]{3,2,1,0:T(8,128)}, u32[]{:S(2)}) copy-start(f32[4,8,8,128]{3,2,1,0:T(8,128)} %param.8) | copy-start | bytes 393220
  3.0 1.1 %copy-start.3 = (f32[8,8,128]{2,1,0:T(8,128)S(1)}, f32[8,8,128]{2,1,0:T(8,128)}, u32[]{:S(2)}) copy-start(f32[8,8,128]{2,1,0:T(8,128)} %param.7) | copy-start | bytes 98308
  3.0 0.8 %copy-start.5 = (s32[1,1,16]{2,1,0:T(1,128)S(1)}, s32[1,1,16]{2,1,0:T(1,128)}, u32[]{:S(2)}) copy-start(s32[1,1,16]{2,1,0:T(1,128)} %param.9) | copy-start | bytes 196
where the time goes:
time: 47.9 us; the launch traced here: 47.7 us
  Pallas kernels  42.3 us (88%)
  local copies, waits for them, and re-layouts  4.59 us (10%)
  between operations  0.76 us (2%)
    pallas_call x1, Pallas kernels, on_device(): pl.pallas_call(lambda *refs: kernel(counts, *refs), out_shape=(jax.ShapeD...  42.3 us
    unnamed x17, local copies, waits for them, and re-layouts  2.97 us
    slice x1, local copies, waits for them, and re-layouts, on_device(): turned[2]  1.43 us

commit v1 on v0

--- a/solution.py
+++ b/solution.py
@@ -83,22 +83,12 @@
         pack_scatter[row, slot_row(x, y)] = 1
     for row, x, y in message_rows(scatter_to):
         unpack_scatter[node_row(x, y), 160 + row] = 1
-    depth = np.zeros((64, 256))
-    for row, lane in enumerate((126, 127, 1, 0)):
-        depth[row, lane] = 1
-    for row, lane in ((0, 128), (1, 0), (10, 129), (11, 127)):
-        depth[16 + row, lane] = 1
-    for row, lane in enumerate((129, 127, 128, 0)):
-        depth[32 + row, lane] = 1
-    for row, lane in ((0, 1), (1, 0), (10, 126), (11, 127)):
-        depth[48 + row, lane] = 1
-    table = np.zeros((480, 256))
+    table = np.zeros((416, 256))
     for start, part in (
         (0, pack_gather),
         (96, unpack_gather),
         (256, pack_scatter),
         (352, unpack_scatter),
-        (416, depth),
     ):
         table[start : start + part.shape[0], : part.shape[1]] = part
     return table
@@ -108,12 +98,12 @@
     derivative = derivative_table()
     eye = np.eye(8)
     plane = np.concatenate([np.kron(derivative, eye), np.kron(eye, derivative)], 0)
-    deep = np.kron(np.eye(16), derivative)
-    table = np.zeros((448, 128))
+    deep = np.kron(np.eye(32), derivative)
+    table = np.zeros((704, 256))
     table[0:128, :64] = plane
-    table[128:192] = plane.T
-    table[192:320] = deep.T
-    table[320:448] = deep
+    table[128:192, :128] = plane.T
+    table[192:448] = deep.T
+    table[448:704] = deep
     return table
 
 
@@ -151,8 +141,10 @@
     derive_ref,
     solution_ref,
     residual_ref,
-    deep_send,
-    deep_recv,
+    right_recv,
+    geometry_recv,
+    class_recv,
+    wide_geometry,
     plane_send,
     plane_recv,
     first_ref,
@@ -175,9 +167,10 @@
     plane_size = nx * ny
     me_plane = gx * ny + gy
 
-    deep_recv[...] = jnp.zeros_like(deep_recv)
+    right_recv[...] = jnp.zeros_like(right_recv)
+    geometry_recv[...] = jnp.zeros_like(geometry_recv)
+    class_recv[...] = jnp.zeros_like(class_recv)
     plane_recv[...] = jnp.zeros_like(plane_recv)
-    deep_send[...] = jnp.zeros_like(deep_send)
 
     def plane_partner(offset):
         other = lax.rem(me_plane + offset, plane_size)
@@ -196,11 +189,18 @@
         pl.semaphore_signal(barrier, inc=1, device_id=line_partner(offset)[1], device_id_type=MESH)
     pl.semaphore_wait(barrier, plane_size + nz - 2)
 
+    inputs = (
+        (right_ref, right_recv),
+        (class_ref, class_recv),
+        (geometry_ref, geometry_recv),
+    )
+
     def deep_copy(number, step):
         side = 0 if step > 0 else 1
+        mine, theirs = inputs[number]
         return pltpu.make_async_remote_copy(
-            src_ref=deep_send.at[number],
-            dst_ref=deep_recv.at[number, pl.ds(8 * side, 8)],
+            src_ref=mine,
+            dst_ref=theirs.at[side],
             send_sem=deep_sems.at[0, number, side],
             recv_sem=deep_sems.at[1, number, side],
             device_id=(gx, gy, gz + step),
@@ -210,15 +210,17 @@
     def deep_exists(step):
         return gz + 1 < nz if step > 0 else gz > 0
 
-    def deep_start(number, message):
-        deep_send[number, :, 0:64] = message
+    def deep_start(number):
         for step in (1, -1):
             pl.when(deep_exists(step))(lambda step=step: deep_copy(number, step).start())
 
     def deep_wait(number):
         for step in (1, -1):
             pl.when(deep_exists(-step))(lambda step=step: deep_copy(number, step).wait_recv())
-        return deep_recv[number][:, 0:64]
+
+    def widen(own, received):
+        half = lax.broadcasted_iota(jnp.int32, own.shape, 1) < 64
+        return jnp.concatenate([own, jnp.where(half, received[1], received[0])], 1)
 
     def plane_copy(number, at):
         dx, dy = DIRECTIONS[at]
@@ -248,19 +250,14 @@
 
     rows = lax.broadcasted_iota(jnp.int32, (64, 128), 0)
     lanes = lax.broadcasted_iota(jnp.int32, (64, 128), 1)
+    plain = ((1,), (0,))
     rows_rows = ((1,), (1,))
-    plain = ((1,), (0,))
-    columns = ((0,), (0,))
-
-    def gather_deep_start(number, field):
-        deep_start(number, pick(select_ref[416:424, 0:128], field, rows_rows))
-
-    def gather_deep_end(number, field):
-        node = lax.rem(lanes, 8)
-        following = jnp.where((node == 7) & (lanes < 127), pltpu.roll(field, 127, 1), 0.0)
-        previous = jnp.where((node == 0) & (lanes > 0), pltpu.roll(field, 1, 1), 0.0)
-        wide = jnp.concatenate([field + following + previous, jnp.zeros_like(field)], 1)
-        return wide + place(deep_wait(number), select_ref[432:448, :], columns)
+
+    def sum_deep(field):
+        node = lax.rem(lax.broadcasted_iota(jnp.int32, (64, 256), 1), 8)
+        following = jnp.where(node == 7, pltpu.roll(field, 255, 1), 0.0)
+        previous = jnp.where(node == 0, pltpu.roll(field, 1, 1), 0.0)
+        return field + following + previous
 
     def gather_plane_start(number, wide):
         plane_start(number, pick(select_ref[0:96, 0:64], wide, plain))
@@ -272,9 +269,7 @@
     def scatter(number, extended):
         plane_start(number, pick(select_ref[256:352, 0:160], extended, plain))
         both = jnp.concatenate([extended, plane_wait(number)], 0)
-        wide = pick(select_ref[352:416, :], both, plain)
-        deep_start(number, pick(select_ref[448:456, :], wide, rows_rows))
-        return wide[:, 0:128] + place(deep_wait(number), select_ref[464:480, 0:128], columns)
+        return pick(select_ref[352:416, :], both, plain)
 
     def solve(extended):
         value = jnp.dot(extended, third_ref[...], precision=HIGHEST).reshape(10, 16, 256)
@@ -299,10 +294,12 @@
 
     def local(field):
         slopes = jnp.dot(derive_ref[0:128, 0:64], field, precision=HIGHEST)
-        deep = jnp.dot(field, derive_ref[192:320, :], precision=HIGHEST)
-        back = jnp.dot(derive_ref[128:192, :], geometry_ref[0:128] * slopes, precision=HIGHEST)
-        deep = jnp.dot(geometry_ref[128:192] * deep, derive_ref[320:448, :], precision=HIGHEST)
-        return back + deep + geometry_ref[192:256] * field
+        deep = jnp.dot(field, derive_ref[192:448, :], precision=HIGHEST)
+        back = jnp.dot(
+            derive_ref[128:192, 0:128], wide_geometry[0:128] * slopes, precision=HIGHEST
+        )
+        deep = jnp.dot(wide_geometry[128:192] * deep, derive_ref[448:704, :], precision=HIGHEST)
+        return back + deep + wide_geometry[192:256] * field
 
     def factor(inside, length, device, devices):
         last = (device == devices - 1) & (inside == length - 1)
@@ -311,41 +308,62 @@
         shared = ((node == 7) & ~last) | ((node == 0) & ~first)
         return jnp.where(shared, 0.5, 1.0).astype(F32)
 
-    weight = (
-        factor(rows // 8, 8, gx, nx) * factor(lax.rem(rows, 8), 8, gy, ny)
-        * factor(lanes, 128, gz, nz)
-    )
+    plane_weight = factor(rows // 8, 8, gx, nx) * factor(lax.rem(rows, 8), 8, gy, ny)
+    weight = plane_weight * factor(lanes, 128, gz, nz)
     right = right_ref[...]
     weighted = weight * right
-    gather_deep_start(0, weighted)
-
-    classes = class_ref[...]
-    chooser = (lax.broadcasted_iota(jnp.int32, (32, 256), 0) == classes).astype(F32).astype(BF16)
+    for number in range(3):
+        deep_start(number)
+    deep_wait(0)
+    wide = jnp.concatenate([plane_weight, plane_weight], 1) * widen(right, right_recv[...])
+    gather_plane_start(0, wide)
+    deep_wait(1)
+
+    def element_of(shape):
+        place_at = lax.rem(lax.broadcasted_iota(jnp.int32, shape, 1), 24)
+        return jnp.where(place_at < 20, place_at, place_at - 24)
+
+    source = lax.broadcasted_iota(jnp.int32, (384, 256), 0)
+    source = jnp.where(source < 128, source, jnp.where(source < 256, source - 112, source - 272))
+    known = jnp.concatenate([class_ref[...], class_recv[1], class_recv[0]], 1).astype(BF16)
+    classes = jnp.dot(
+        known,
+        (source == element_of((384, 256))).astype(F32).astype(BF16),
+        preferred_element_type=F32,
+    )[0:1]
+    kind = lax.broadcasted_iota(jnp.int32, (32, 256), 0).astype(F32)
+    chooser = (jnp.abs(kind - classes) < 0.5).astype(F32).astype(BF16)
     table = place(table_ref[...], chooser, plain)
     for a in range(10):
         for m in range(10):
             first_ref[a, m] = jnp.broadcast_to(table[a * 10 + m : a * 10 + m + 1], (16, 256))
     second_ref[...] = table[104:264].reshape(10, 16, 256)
     second_back_ref[...] = table[264:424].reshape(10, 16, 256)
-    mode = lax.broadcasted_iota(jnp.int32, (1, 256), 1) // 16
+    mode = lax.broadcasted_iota(jnp.int32, (1, 256), 1) // 24
     third = jnp.zeros((16, 256), F32)
     level = jnp.zeros((1, 256), F32)
     for p in range(10):
         third = third + jnp.where(mode == p, table[424 + 16 * p : 440 + 16 * p], 0.0)
         level = level + jnp.where(mode == p, table[616 + p : 617 + p], 0.0)
 
-    wide = gather_deep_end(0, weighted)
-    gather_plane_start(0, wide)
-
     for m in range(10):
         inverse_ref[m] = 1.0 / (table[600 + m : 601 + m] + table[584:600] + level)
     node = lax.broadcasted_iota(jnp.int32, (256, 256), 0)
-    element = lax.rem(lax.broadcasted_iota(jnp.int32, (256, 256), 1), 16)
-    reach = jnp.where(node == 128, -2, node) - 8 * element
+    node = jnp.where(node < 192, node, node - 256)
+    element = element_of((256, 256))
+    reach = node - 8 * element
     slot = jnp.where(
         reach == -2, 0, jnp.where(reach == 9, 9, jnp.where((reach >= 0) & (reach < 8), reach + 1, -1))
     )
     slot_back = jnp.where(reach == 8, 8, jnp.where(reach == -1, 1, slot))
+    inside = (
+        (16 * gz + element >= 0)
+        & (16 * gz + element < 16 * nz)
+        & (128 * gz + node >= 0)
+        & (128 * gz + node < 128 * nz)
+    )
+    slot = jnp.where(inside, slot, -1)
+    slot_back = jnp.where(inside, slot_back, -1)
     spread = jnp.zeros((256, 256), F32)
     spread_back = jnp.zeros((256, 256), F32)
     for c in range(10):
@@ -355,25 +373,27 @@
     third_back_ref[...] = spread_back
 
     extended = gather_plane_end(0, wide)
-    precond = scatter(1, solve(extended))
-    image_local = local(precond)
-    gather_deep_start(2, image_local)
-    wide = gather_deep_end(2, image_local)
+    wide_precond = scatter(1, solve(extended))
+    deep_wait(2)
+    wide_geometry[...] = widen(geometry_ref[...], geometry_recv[...])
+    image_local = local(wide_precond)
+    wide = sum_deep(image_local)
     gather_plane_start(2, wide)
     extended = gather_plane_end(2, wide)
     image = jnp.concatenate(
         [extended[16 * x + 1 : 16 * x + 9, 0:128] for x in range(1, 9)], 0
     )
-    again = scatter(3, solve(extended))
-    again_local = local(again)
+    wide_again = scatter(3, solve(extended))
+    again_local = local(wide_again)
+    precond, again = wide_precond[:, 0:128], wide_again[:, 0:128]
 
     products = (
         weighted * precond,
-        precond * image_local,
+        precond * image_local[:, 0:128],
         weighted * again,
         weight * image * again,
-        precond * again_local,
-        again * again_local,
+        precond * again_local[:, 0:128],
+        again * again_local[:, 0:128],
     )
     kind = lax.broadcasted_iota(jnp.int32, (8, 128), 0)
     packed = jnp.zeros((8, 128), F32)
@@ -398,8 +418,7 @@
         sum_copy(
             sums_plane, sum_send_sems, sum_plane_sems, offset, me_plane, plane_partner(offset)[1]
         ).start()
-    gather_deep_start(4, again_local)
-    wide = gather_deep_end(4, again_local)
+    wide = sum_deep(again_local)
     gather_plane_start(4, wide)
     for offset in range(1, plane_size):
         sum_wait(sums_plane, sum_plane_sems, plane_partner(offset)[0])
@@ -426,11 +445,12 @@
     solution_ref[...] = on_precond * precond - on_again * again
     residual_ref[...] = right - on_precond * image + on_again * again_image
 
-    for number in range(ROUNDS):
+    for number in range(3):
         for step in (1, -1):
             pl.when(deep_exists(step))(
                 lambda number=number, step=step: deep_copy(number, step).wait_send()
             )
+    for number in range(ROUNDS):
         for at, (dx, dy) in enumerate(DIRECTIONS):
             pl.when(plane_exists(dx, dy))(
                 lambda number=number, at=at: plane_copy(number, at).wait_send()
@@ -448,7 +468,7 @@
 def on_device(counts, right_side, geometry, element_shape_class, fdm_vectors, fdm_values):
     nx, ny, nz = counts
     shape = right_side.shape
-    classes = jnp.tile(element_shape_class.reshape(1, 16), (1, 16))
+    classes = jnp.pad(element_shape_class.reshape(1, 16).astype(F32), ((0, 7), (0, 112)))
     turned = jnp.transpose(fdm_vectors, (1, 2, 3, 0))
     levels = jnp.transpose(fdm_values, (1, 2, 0))
 
@@ -475,8 +495,10 @@
         in_specs=[vmem] * 6,
         out_specs=(vmem, vmem),
         scratch_shapes=[
-            pltpu.VMEM((ROUNDS, 8, 128), F32),
-            pltpu.VMEM((ROUNDS, 16, 128), F32),
+            pltpu.VMEM((2, 64, 128), F32),
+            pltpu.VMEM((2, 256, 128), F32),
+            pltpu.VMEM((2, 8, 128), F32),
+            pltpu.VMEM((256, 256), F32),
             pltpu.VMEM((ROUNDS, 96, 256), F32),
             pltpu.VMEM((ROUNDS, 96, 256), F32),
             pltpu.VMEM((10, 10, 16, 256), F32),
@@ -487,7 +509,7 @@
             pltpu.VMEM((10, 16, 256), F32),
             pltpu.VMEM((nx * ny, 8, 128), F32),
             pltpu.VMEM((nz, 8, 128), F32),
-            pltpu.SemaphoreType.DMA((2, ROUNDS, 2)),
+            pltpu.SemaphoreType.DMA((2, 3, 2)),
             pltpu.SemaphoreType.DMA((2, ROUNDS, 8)),
             pltpu.SemaphoreType.DMA((nx * ny,)),
             pltpu.SemaphoreType.DMA((nx * ny,)),

time: 47.9 us -> 39.2 us (0.82)
  Pallas kernels: 42.3 us -> 33.9 us
    pallas_call x1, Pallas kernels: 42.3 us -> 33.9 us  [on_device(): pl.pallas_call(lambda *refs: kernel(counts, *refs), out_shape=(jax.ShapeD...]
where the time goes in v1:
time: 39.2 us; the launch traced here: 39.1 us
  Pallas kernels  33.9 us (86%)
  local copies, waits for them, and re-layouts  4.4 us (11%)
  between operations  0.76 us (2%)
    pallas_call x1, Pallas kernels, on_device(): pl.pallas_call(lambda *refs: kernel(counts, *refs), out_shape=(jax.ShapeD...  33.9 us
    unnamed x17, local copies, waits for them, and re-layouts  2.85 us
    slice x1, local copies, waits for them, and re-layouts, on_device(): turned[2]  1.43 us

profile of v1, /device:TPU:0, one launch (start us, length us, event | category | flops | bytes accessed | tf_op | source)
XLA Modules:
  0.0 39.1 jit_solution(4002337580493058407)
XLA Ops:
  0.6 1.4 %fusion = (f32[1,10,10,32]{3,0,2,1:T(1,128)S(1)}, f32[1,10,10,32]{3,0,2,1:T(1,128)S(1)}, f32[10,10,32]{2,1,0:T(8,128)S(1)}) fusion(f32[3,10,10,32]{3,0,2,1:T(4,128)} %bitcast.39), kind=kLoop, calls=%fused_computation.9 | loop fusion | bytes 76800 | tf_op jit(solution)/shard_map/slice | solution.py:484
  2.1 0.0 copy-start.4
  2.1 0.0 copy-start
  2.2 0.6 %copy-done.4 = f32[32,3,10]{0,1,2:T(4,128)S(1)} copy-done((f32[32,3,10]{0,1,2:T(4,128)S(1)}, f32[32,3,10]{0,1,2:T(4,128)}, u32[]{:S(2)}) %copy-start.4) | copy-done | bytes 3864
  2.9 0.0 copy-start.5
  2.9 0.0 copy-start.1
  2.9 0.0 copy-start.2
  2.9 0.0 copy-start.3
  3.0 0.6 %copy-done.5 = s32[1,1,16]{2,1,0:T(1,128)S(1)} copy-done((s32[1,1,16]{2,1,0:T(1,128)S(1)}, s32[1,1,16]{2,1,0:T(1,128)}, u32[]{:S(2)}) %copy-start.5) | copy-done | bytes 88
  3.5 0.0 copy-done
  3.5 0.3 copy-done.1
  3.9 0.0 copy-done.2
  3.9 0.0 copy-done.3
  3.9 33.9 %shard_map.86 = (f32[64,128]{1,0:T(8,128)S(1)}, f32[64,128]{1,0:T(8,128)S(1)}) custom-call(f32[64,128]{1,0:T(8,128)S(1)} %bitcast.32, f32[256,128]{1,0:T(8,128)S(1)} %bitcast.31, f32[8,128]{1,0:T(8,128)S(1)} %pad.24.refs_2_, f32[632,32]{1,0:T(8,128)S(1)} %concatenate.3.refs_3_, bf16[416,256]{1,0:T(8,128)(2,1)S(1)} %copy-done.1, f32[704,256]{1,0:T(8,128)S(1)} %copy-done), custom_call_target="tpu_custom_call" | custom-call | tf_op jit(solution)/shard_map/pallas_call | solution.py:492
  37.8 0.6 %copy.47 = f32[8,8,128]{2,1,0:T(8,128)} copy(f32[8,8,128]{2,1,0:T(8,128)S(1)} %bitcast.34) | data formatting | bytes 65536
  38.4 0.6 %copy.48 = f32[8,8,128]{2,1,0:T(8,128)} copy(f32[8,8,128]{2,1,0:T(8,128)S(1)} %bitcast.33) | data formatting | bytes 65536
  (15 shorter events, 0.1 us)
Async XLA Ops:
  2.1 0.7 %copy-start.4 = (f32[32,3,10]{0,1,2:T(4,128)S(1)}, f32[32,3,10]{0,1,2:T(4,128)}, u32[]{:S(2)}) copy-start(f32[32,3,10]{0,1,2:T(4,128)} %param.11) | copy-start | bytes 11524
  2.1 1.4 %copy-start = (f32[704,256]{1,0:T(8,128)S(1)}, f32[704,256]{1,0:T(8,128)}, u32[]{:S(2)}) copy-start(f32[704,256]{1,0:T(8,128)} %constant.9.clone.refs_5_) | copy-start | bytes 2162692
  2.9 0.7 %copy-start.5 = (s32[1,1,16]{2,1,0:T(1,128)S(1)}, s32[1,1,16]{2,1,0:T(1,128)}, u32[]{:S(2)}) copy-start(s32[1,1,16]{2,1,0:T(1,128)} %param.9) | copy-start | bytes 196
  2.9 1.0 %copy-start.1 = (bf16[416,256]{1,0:T(8,128)(2,1)S(1)}, bf16[416,256]{1,0:T(8,128)(2,1)}, u32[]{:S(2)}) copy-start(bf16[416,256]{1,0:T(8,128)(2,1)} %constant.8.clone.refs_4_) | copy-start | bytes 638980
  2.9 1.0 %copy-start.2 = (f32[4,8,8,128]{3,2,1,0:T(8,128)S(1)}, f32[4,8,8,128]{3,2,1,0:T(8,128)}, u32[]{:S(2)}) copy-start(f32[4,8,8,128]{3,2,1,0:T(8,128)} %param.8) | copy-start | bytes 393220
  2.9 1.0 %copy-start.3 = (f32[8,8,128]{2,1,0:T(8,128)S(1)}, f32[8,8,128]{2,1,0:T(8,128)}, u32[]{:S(2)}) copy-start(f32[8,8,128]{2,1,0:T(8,128)} %param.7) | copy-start | bytes 98308

commit v2 on v1

--- a/solution.py
+++ b/solution.py
@@ -6,7 +6,6 @@
 from jax.experimental.pallas import tpu as pltpu
 from jax.sharding import PartitionSpec as P
 
-HIGHEST = lax.Precision.HIGHEST
 MESH = pl.DeviceIdType.MESH
 F32 = jnp.float32
 BF16 = jnp.bfloat16
@@ -67,7 +66,7 @@
     gather_to = {1: (0, 1), -1: (9, 8)}
     scatter_from = {1: (9, 8), -1: (0, 1)}
     scatter_to = {1: (2, 1), -1: (7, 8)}
-    pack_gather = np.zeros((96, 64))
+    pack_gather = np.zeros((96, 128))
     unpack_gather = np.zeros((160, 160))
     pack_scatter = np.zeros((96, 160))
     unpack_scatter = np.zeros((64, 256))
@@ -76,34 +75,28 @@
             unpack_gather[slot_row(x, y), node_row(x, y)] = 1
             unpack_scatter[node_row(x, y), slot_row(x, y)] = 1
     for row, x, y in message_rows(gather_from):
-        pack_gather[row, node_row(x, y)] = 1
+        pack_gather[row, [node_row(x, y), 64 + node_row(x, y)]] = 1
     for row, x, y in message_rows(gather_to):
         unpack_gather[slot_row(x, y), 64 + row] = 1
     for row, x, y in message_rows(scatter_from):
         pack_scatter[row, slot_row(x, y)] = 1
     for row, x, y in message_rows(scatter_to):
         unpack_scatter[node_row(x, y), 160 + row] = 1
-    table = np.zeros((416, 256))
+    derivative = derivative_table()
+    eye = np.eye(8)
+    plane = np.concatenate([np.kron(derivative, eye), np.kron(eye, derivative)], 0)
+    high = np.asarray(np.asarray(plane, BF16), np.float64)
+    low = plane - high
+    table = np.zeros((608, 256))
     for start, part in (
         (0, pack_gather),
         (96, unpack_gather),
         (256, pack_scatter),
         (352, unpack_scatter),
+        (416, np.concatenate([high, high, low], 1)),
+        (544, np.concatenate([high.T, low.T], 1)),
     ):
         table[start : start + part.shape[0], : part.shape[1]] = part
-    return table
-
-
-def derivative_matrices():
-    derivative = derivative_table()
-    eye = np.eye(8)
-    plane = np.concatenate([np.kron(derivative, eye), np.kron(eye, derivative)], 0)
-    deep = np.kron(np.eye(32), derivative)
-    table = np.zeros((704, 256))
-    table[0:128, :64] = plane
-    table[128:192, :128] = plane.T
-    table[192:448] = deep.T
-    table[448:704] = deep
     return table
 
 
@@ -115,12 +108,27 @@
     return low, middle, high
 
 
-def pick(chooser, value, dims):
-    total = None
-    for piece in pieces(value):
-        part = lax.dot_general(chooser, piece, (dims, ((), ())), preferred_element_type=F32)
-        total = part if total is None else total + part
-    return total
+def halves(value):
+    high = value.astype(BF16)
+    return high, (value - high.astype(F32)).astype(BF16)
+
+
+def product(left, right, dims=((1,), (0,))):
+    return lax.dot_general(left, right, (dims, ((), ())), preferred_element_type=F32)
+
+
+def pick(chooser, value):
+    high, low = halves(value)
+    return product(chooser, low) + product(chooser, high)
+
+
+def times(value, high_ref, low_ref, dims=((1,), (0,))):
+    high, low = halves(value)
+    return (
+        product(low, high_ref[...], dims)
+        + product(high, low_ref[...], dims)
+        + product(high, high_ref[...], dims)
+    )
 
 
 def place(value, chooser, dims):
@@ -135,23 +143,28 @@
     counts,
     right_ref,
     geometry_ref,
-    class_ref,
-    table_ref,
+    element_ref,
+    vectors_ref,
+    values_ref,
     select_ref,
-    derive_ref,
-    solution_ref,
-    residual_ref,
+    deep_ref,
+    result_ref,
     right_recv,
     geometry_recv,
     class_recv,
     wide_geometry,
+    class_ref,
+    deep_high,
+    deep_low,
     plane_send,
     plane_recv,
     first_ref,
     second_ref,
     second_back_ref,
-    third_ref,
-    third_back_ref,
+    third_high,
+    third_low,
+    back_high,
+    back_low,
     inverse_ref,
     sums_plane,
     sums_line,
@@ -180,6 +193,9 @@
         other = lax.rem(gz + offset, nz)
         return other, (gx, gy, other)
 
+    class_ref[...] = jnp.zeros_like(class_ref)
+    class_ref[0:1, 0:16] = element_ref[...].astype(F32)
+
     barrier = pltpu.get_barrier_semaphore()
     for offset in range(1, plane_size):
         pl.semaphore_signal(
@@ -260,19 +276,19 @@
         return field + following + previous
 
     def gather_plane_start(number, wide):
-        plane_start(number, pick(select_ref[0:96, 0:64], wide, plain))
+        plane_start(number, product(select_ref[0:96, 0:128], jnp.concatenate(halves(wide), 0)))
 
     def gather_plane_end(number, wide):
         both = jnp.concatenate([wide, plane_wait(number)], 0)
-        return pick(select_ref[96:256, 0:160], both, plain)
+        return pick(select_ref[96:256, 0:160], both)
 
     def scatter(number, extended):
-        plane_start(number, pick(select_ref[256:352, 0:160], extended, plain))
+        plane_start(number, pick(select_ref[256:352, 0:160], extended))
         both = jnp.concatenate([extended, plane_wait(number)], 0)
-        return pick(select_ref[352:416, :], both, plain)
+        return pick(select_ref[352:416, :], both)
 
     def solve(extended):
-        value = jnp.dot(extended, third_ref[...], precision=HIGHEST).reshape(10, 16, 256)
+        value = times(extended, third_high, third_low).reshape(10, 16, 256)
         total = first_ref[0] * value[0][None]
         for a in range(1, 10):
             total = total + first_ref[a] * value[a][None]
@@ -288,17 +304,21 @@
         total = first_ref[:, 0] * value[0][None]
         for m in range(1, 10):
             total = total + first_ref[:, m] * value[m][None]
-        return lax.dot_general(
-            total.reshape(160, 256), third_back_ref[...], (rows_rows, ((), ())), precision=HIGHEST
+        return times(total.reshape(160, 256), back_high, back_low, rows_rows)
+
+    def slopes_of(field):
+        high, low = halves(field)
+        slopes = product(select_ref[416:544, 0:192], jnp.concatenate([high, low, high], 0))
+        return slopes, times(field, deep_high, deep_low)
+
+    def local(field, slopes, deep):
+        high, low = halves(wide_geometry[0:128] * slopes)
+        back = (
+            product(select_ref[544:608, 0:128], low)
+            + product(select_ref[544:608, 128:256], high)
+            + product(select_ref[544:608, 0:128], high)
         )
-
-    def local(field):
-        slopes = jnp.dot(derive_ref[0:128, 0:64], field, precision=HIGHEST)
-        deep = jnp.dot(field, derive_ref[192:448, :], precision=HIGHEST)
-        back = jnp.dot(
-            derive_ref[128:192, 0:128], wide_geometry[0:128] * slopes, precision=HIGHEST
-        )
-        deep = jnp.dot(wide_geometry[128:192] * deep, derive_ref[448:704, :], precision=HIGHEST)
+        deep = times(wide_geometry[128:192] * deep, deep_high, deep_low, rows_rows)
         return back + deep + wide_geometry[192:256] * field
 
     def factor(inside, length, device, devices):
@@ -314,6 +334,21 @@
     weighted = weight * right
     for number in range(3):
         deep_start(number)
+
+    blank = jnp.zeros((6, 32), F32)
+    groups = (
+        [vectors_ref[a, :, 0, :] for a in range(10)]
+        + [vectors_ref[b, :, 1, :] for b in range(10)]
+        + [vectors_ref[:, n, 1, :] for n in range(10)]
+        + [vectors_ref[:, p, 2, :] for p in range(10)]
+        + [values_ref[:, d, :] for d in (1, 0, 2)]
+    )
+    entries = jnp.concatenate([part for group in groups for part in (group, blank)], 0)
+    corner = lax.broadcasted_iota(jnp.int32, (256, 256), 0) // 8
+    along = lax.broadcasted_iota(jnp.int32, (256, 256), 1) // 8
+    high, low = halves(jnp.where(corner == along, jnp.concatenate([deep_ref[...]] * 32, 0), 0.0))
+    deep_high[...] = high
+    deep_low[...] = low
     deep_wait(0)
     wide = jnp.concatenate([plane_weight, plane_weight], 1) * widen(right, right_recv[...])
     gather_plane_start(0, wide)
@@ -333,21 +368,21 @@
     )[0:1]
     kind = lax.broadcasted_iota(jnp.int32, (32, 256), 0).astype(F32)
     chooser = (jnp.abs(kind - classes) < 0.5).astype(F32).astype(BF16)
-    table = place(table_ref[...], chooser, plain)
+    table = place(entries, chooser, plain)
     for a in range(10):
         for m in range(10):
-            first_ref[a, m] = jnp.broadcast_to(table[a * 10 + m : a * 10 + m + 1], (16, 256))
-    second_ref[...] = table[104:264].reshape(10, 16, 256)
-    second_back_ref[...] = table[264:424].reshape(10, 16, 256)
+            first_ref[a, m] = jnp.broadcast_to(table[a * 16 + m : a * 16 + m + 1], (16, 256))
+    second_ref[...] = table[160:320].reshape(10, 16, 256)
+    second_back_ref[...] = table[320:480].reshape(10, 16, 256)
     mode = lax.broadcasted_iota(jnp.int32, (1, 256), 1) // 24
     third = jnp.zeros((16, 256), F32)
     level = jnp.zeros((1, 256), F32)
     for p in range(10):
-        third = third + jnp.where(mode == p, table[424 + 16 * p : 440 + 16 * p], 0.0)
-        level = level + jnp.where(mode == p, table[616 + p : 617 + p], 0.0)
+        third = third + jnp.where(mode == p, table[480 + 16 * p : 496 + 16 * p], 0.0)
+        level = level + jnp.where(mode == p, table[672 + p : 673 + p], 0.0)
 
     for m in range(10):
-        inverse_ref[m] = 1.0 / (table[600 + m : 601 + m] + table[584:600] + level)
+        inverse_ref[m] = 1.0 / (table[656 + m : 657 + m] + table[640:656] + level)
     node = lax.broadcasted_iota(jnp.int32, (256, 256), 0)
     node = jnp.where(node < 192, node, node - 256)
     element = element_of((256, 256))
@@ -369,14 +404,14 @@
     for c in range(10):
         spread = jnp.where(slot == c, third[c : c + 1], spread)
         spread_back = jnp.where(slot_back == c, third[c : c + 1], spread_back)
-    third_ref[...] = spread
-    third_back_ref[...] = spread_back
+    third_high[...], third_low[...] = halves(spread)
+    back_high[...], back_low[...] = halves(spread_back)
 
     extended = gather_plane_end(0, wide)
     wide_precond = scatter(1, solve(extended))
     deep_wait(2)
     wide_geometry[...] = widen(geometry_ref[...], geometry_recv[...])
-    image_local = local(wide_precond)
+    image_local = local(wide_precond, *slopes_of(wide_precond))
     wide = sum_deep(image_local)
     gather_plane_start(2, wide)
     extended = gather_plane_end(2, wide)
@@ -384,21 +419,27 @@
         [extended[16 * x + 1 : 16 * x + 9, 0:128] for x in range(1, 9)], 0
     )
     wide_again = scatter(3, solve(extended))
-    again_local = local(wide_again)
+    slopes, deep = slopes_of(wide_again)
     precond, again = wide_precond[:, 0:128], wide_again[:, 0:128]
 
+    own = geometry_ref[...]
+    energy = (
+        own[0:64] * slopes[0:64, 0:128] * slopes[0:64, 0:128]
+        + own[64:128] * slopes[64:128, 0:128] * slopes[64:128, 0:128]
+        + own[128:192] * deep[:, 0:128] * deep[:, 0:128]
+        + own[192:256] * again * again
+    )
     products = (
         weighted * precond,
         precond * image_local[:, 0:128],
         weighted * again,
         weight * image * again,
-        precond * again_local[:, 0:128],
-        again * again_local[:, 0:128],
+        energy,
     )
     kind = lax.broadcasted_iota(jnp.int32, (8, 128), 0)
     packed = jnp.zeros((8, 128), F32)
-    for number, product in enumerate(products):
-        packed = packed + jnp.where(kind == number, jnp.sum(product, 0, keepdims=True), 0.0)
+    for number, entry in enumerate(products):
+        packed = packed + jnp.where(kind == number, jnp.sum(entry, 0, keepdims=True), 0.0)
 
     def sum_copy(buffer, send_sems, recv_sems, offset, mine, partner):
         return pltpu.make_async_remote_copy(
@@ -418,7 +459,7 @@
         sum_copy(
             sums_plane, sum_send_sems, sum_plane_sems, offset, me_plane, plane_partner(offset)[1]
         ).start()
-    wide = sum_deep(again_local)
+    wide = sum_deep(local(wide_again, slopes, deep))
     gather_plane_start(4, wide)
     for offset in range(1, plane_size):
         sum_wait(sums_plane, sum_plane_sems, plane_partner(offset)[0])
@@ -434,16 +475,16 @@
     for offset in range(1, nz):
         sum_wait(sums_line, sum_line_sems, line_partner(offset)[0])
     sums = jnp.sum(jnp.sum(sums_line[...], 0), 1, keepdims=True)
-    a, b, c, d, e, f = [sums[k : k + 1] for k in range(6)]
+    a, b, c, d, f = [sums[k : k + 1] for k in range(5)]
     step_one = a / b
     rho = a - step_one * (b + c) + step_one * step_one * d
     stretch = 1.0 + rho / a
-    curvature = stretch * stretch * b - stretch * step_one * (d + e) + step_one * step_one * f
+    curvature = stretch * stretch * b - 2.0 * stretch * step_one * d + step_one * step_one * f
     step_two = rho / curvature
     on_precond = step_one + step_two * stretch
     on_again = step_one * step_two
-    solution_ref[...] = on_precond * precond - on_again * again
-    residual_ref[...] = right - on_precond * image + on_again * again_image
+    result_ref[0] = on_precond * precond - on_again * again
+    result_ref[1] = right - on_precond * image + on_again * again_image
 
     for number in range(3):
         for step in (1, -1):
@@ -468,44 +509,29 @@
 def on_device(counts, right_side, geometry, element_shape_class, fdm_vectors, fdm_values):
     nx, ny, nz = counts
     shape = right_side.shape
-    classes = jnp.pad(element_shape_class.reshape(1, 16).astype(F32), ((0, 7), (0, 112)))
-    turned = jnp.transpose(fdm_vectors, (1, 2, 3, 0))
-    levels = jnp.transpose(fdm_values, (1, 2, 0))
-
-    def padded(part):
-        return jnp.pad(part, ((0, 0), (0, 6), (0, 0))).reshape(160, 32)
-
-    table = jnp.concatenate(
-        [
-            turned[0].reshape(100, 32),
-            jnp.zeros((4, 32), F32),
-            padded(turned[1]),
-            padded(jnp.swapaxes(turned[1], 0, 1)),
-            padded(jnp.swapaxes(turned[2], 0, 1)),
-            jnp.pad(levels[1], ((0, 6), (0, 0))),
-            jnp.pad(levels[0], ((0, 6), (0, 0))),
-            jnp.pad(levels[2], ((0, 6), (0, 0))),
-        ],
-        0,
-    )
     vmem = pl.BlockSpec(memory_space=pltpu.VMEM)
-    solved, left = pl.pallas_call(
+    result = pl.pallas_call(
         lambda *refs: kernel(counts, *refs),
-        out_shape=(jax.ShapeDtypeStruct((64, 128), F32),) * 2,
-        in_specs=[vmem] * 6,
-        out_specs=(vmem, vmem),
+        out_shape=jax.ShapeDtypeStruct((2, 64, 128), F32),
+        in_specs=[vmem] * 7,
+        out_specs=vmem,
         scratch_shapes=[
             pltpu.VMEM((2, 64, 128), F32),
             pltpu.VMEM((2, 256, 128), F32),
             pltpu.VMEM((2, 8, 128), F32),
             pltpu.VMEM((256, 256), F32),
+            pltpu.VMEM((8, 128), F32),
+            pltpu.VMEM((256, 256), BF16),
+            pltpu.VMEM((256, 256), BF16),
             pltpu.VMEM((ROUNDS, 96, 256), F32),
             pltpu.VMEM((ROUNDS, 96, 256), F32),
             pltpu.VMEM((10, 10, 16, 256), F32),
             pltpu.VMEM((10, 16, 256), F32),
             pltpu.VMEM((10, 16, 256), F32),
-            pltpu.VMEM((256, 256), F32),
-            pltpu.VMEM((256, 256), F32),
+            pltpu.VMEM((256, 256), BF16),
+            pltpu.VMEM((256, 256), BF16),
+            pltpu.VMEM((256, 256), BF16),
+            pltpu.VMEM((256, 256), BF16),
             pltpu.VMEM((10, 16, 256), F32),
             pltpu.VMEM((nx * ny, 8, 128), F32),
             pltpu.VMEM((nz, 8, 128), F32),
@@ -522,12 +548,13 @@
     )(
         right_side.reshape(64, 128),
         geometry.reshape(256, 128),
-        classes,
-        table,
+        element_shape_class.reshape(1, 16),
+        jnp.transpose(fdm_vectors, (2, 3, 1, 0)),
+        jnp.transpose(fdm_values, (2, 1, 0)),
         jnp.asarray(selections(), BF16),
-        jnp.asarray(derivative_matrices(), F32),
-    )
-    return solved.reshape(shape), left.reshape(shape)
+        jnp.asarray(np.tile(derivative_table().T, (1, 32)), F32),
+    )
+    return result[0].reshape(shape), result[1].reshape(shape)
 
 
 def solution(mesh):

time: 39.2 us -> 38.8 us (0.990)
  Pallas kernels: 33.9 us -> 32.1 us
  local copies, waits for them, and re-layouts: 4.4 us -> 5.6 us
    unnamed x17 -> x14, local copies, waits for them, and re-layouts: 2.85 us -> 4.97 us
    pallas_call x1, Pallas kernels: 33.9 us -> 32.1 us  [on_device(): pl.pallas_call(lambda *refs: kernel(counts, *refs), out_shape=jax.ShapeDt...]
    slice x1 -> x0, local copies, waits for them, and re-layouts: 1.43 us -> none  [on_device(): turned[2]]
    another operation x1, local copies, waits for them, and re-layouts: 0.01 us -> 0.63 us  [on_device(): return (result[0].reshape(shape), result[1].reshape(shape))]
where the time goes in v2:
time: 38.8 us; the launch traced here: 38.4 us
  Pallas kernels  32.1 us (83%)
  local copies, waits for them, and re-layouts  5.6 us (14%)
  between operations  0.66 us (2%)
    pallas_call x1, Pallas kernels, on_device(): pl.pallas_call(lambda *refs: kernel(counts, *refs), out_shape=jax.ShapeDt...  32.1 us
    unnamed x14, local copies, waits for them, and re-layouts  4.97 us

profile of v2, /device:TPU:0, one launch (start us, length us, event | category | flops | bytes accessed | tf_op | source)
XLA Modules:
  0.0 38.4 jit_solution(14875081804271503790)
XLA Ops:
  0.6 0.0 copy-start.5
  0.6 0.0 copy-start.6
  0.7 0.7 %copy-done.5 = f32[8,256]{1,0:T(8,128)S(1)} copy-done((f32[8,256]{1,0:T(8,128)S(1)}, f32[8,256]{1,0:T(8,128)}, u32[]{:S(2)}) %copy-start.5) | copy-done | bytes 8216
  1.3 0.0 copy-done.6
  1.3 0.0 copy-start
  1.3 1.0 %copy-done = bf16[608,256]{1,0:T(8,128)(2,1)S(1)} copy-done((bf16[608,256]{1,0:T(8,128)(2,1)S(1)}, bf16[608,256]{1,0:T(8,128)(2,1)}, u32[]{:S(2)}) %copy-start) | copy-done | bytes 311320
  2.3 0.0 copy-start.1
  2.3 0.9 %copy-done.1 = f32[32,3,10,10]{0,1,3,2:T(4,128)S(1)} copy-done((f32[32,3,10,10]{0,1,3,2:T(4,128)S(1)}, f32[32,3,10,10]{0,1,3,2:T(4,128)}, u32[]{:S(2)}) %copy-start.1) | copy-done | bytes 38424
  3.2 0.0 copy-start.2
  3.2 0.9 %copy-done.2 = f32[4,8,8,128]{3,2,1,0:T(8,128)S(1)} copy-done((f32[4,8,8,128]{3,2,1,0:T(8,128)S(1)}, f32[4,8,8,128]{3,2,1,0:T(8,128)}, u32[]{:S(2)}) %copy-start.2) | copy-done | bytes 131096
  4.1 0.0 copy-start.3
  4.1 0.8 %copy-done.3 = f32[8,8,128]{2,1,0:T(8,128)S(1)} copy-done((f32[8,8,128]{2,1,0:T(8,128)S(1)}, f32[8,8,128]{2,1,0:T(8,128)}, u32[]{:S(2)}) %copy-start.3) | copy-done | bytes 32792
  4.9 0.0 copy-start.4
  4.9 0.7 %copy-done.4 = f32[32,3,10]{0,1,2:T(4,128)S(1)} copy-done((f32[32,3,10]{0,1,2:T(4,128)S(1)}, f32[32,3,10]{0,1,2:T(4,128)}, u32[]{:S(2)}) %copy-start.4) | copy-done | bytes 3864
  5.6 32.1 %shard_map.86 = f32[2,64,128]{2,1,0:T(8,128)S(1)} custom-call(f32[64,128]{1,0:T(8,128)S(1)} %bitcast.11, f32[256,128]{1,0:T(8,128)S(1)} %bitcast.10, s32[1,16]{1,0:T(1,128)S(1)} %bitcast.13, f32[10,10,3,32]{3,2,1,0:T(4,128)S(1)} %bitcast.9, f32[10,3,32]{2,1,0:T(4,128)S(1)} %bitcast.12, bf16[608,256]{1,0:T(8,128)(2,1)S(1)} %copy-done, f32[8,256]{1,0:T(8,128)S(1)} %copy-done.5), custom_call_target="tpu_custom_call" | custom-call | tf_op jit(solution)/shard_map/pallas_call | solution.py:513
  37.8 0.6 %slice_bitcast_fusion = (f32[8,8,128]{2,1,0:T(8,128)}, f32[8,8,128]{2,1,0:T(8,128)}) fusion(f32[2,64,128]{2,1,0:T(8,128)S(1)} %shard_map.86), kind=kLoop, calls=%fused_computation | loop fusion | bytes 131072 | tf_op jit(solution)/shard_map/reshape;squeeze | solution.py:557
Async XLA Ops:
  0.6 0.7 %copy-start.5 = (f32[8,256]{1,0:T(8,128)S(1)}, f32[8,256]{1,0:T(8,128)}, u32[]{:S(2)}) copy-start(f32[8,256]{1,0:T(8,128)} %constant.5.clone.refs_6_) | copy-start | bytes 24580
  0.6 0.7 %copy-start.6 = (s32[1,1,16]{2,1,0:T(1,128)S(1)}, s32[1,1,16]{2,1,0:T(1,128)}, u32[]{:S(2)}) copy-start(s32[1,1,16]{2,1,0:T(1,128)} %param.9) | copy-start | bytes 196
  1.3 1.0 %copy-start = (bf16[608,256]{1,0:T(8,128)(2,1)S(1)}, bf16[608,256]{1,0:T(8,128)(2,1)}, u32[]{:S(2)}) copy-start(bf16[608,256]{1,0:T(8,128)(2,1)} %constant.4.clone.refs_5_) | copy-start | bytes 933892
  2.3 0.9 %copy-start.1 = (f32[32,3,10,10]{0,1,3,2:T(4,128)S(1)}, f32[32,3,10,10]{0,1,3,2:T(4,128)}, u32[]{:S(2)}) copy-start(f32[32,3,10,10]{0,1,3,2:T(4,128)} %param.10) | copy-start | bytes 115204
  3.2 0.9 %copy-start.2 = (f32[4,8,8,128]{3,2,1,0:T(8,128)S(1)}, f32[4,8,8,128]{3,2,1,0:T(8,128)}, u32[]{:S(2)}) copy-start(f32[4,8,8,128]{3,2,1,0:T(8,128)} %param.8) | copy-start | bytes 393220
  4.1 0.8 %copy-start.3 = (f32[8,8,128]{2,1,0:T(8,128)S(1)}, f32[8,8,128]{2,1,0:T(8,128)}, u32[]{:S(2)}) copy-start(f32[8,8,128]{2,1,0:T(8,128)} %param.7) | copy-start | bytes 98308
  4.9 0.7 %copy-start.4 = (f32[32,3,10]{0,1,2:T(4,128)S(1)}, f32[32,3,10]{0,1,2:T(4,128)}, u32[]{:S(2)}) copy-start(f32[32,3,10]{0,1,2:T(4,128)} %param.11) | copy-start | bytes 11524

commit v3 on v2

--- a/solution.py
+++ b/solution.py
@@ -12,6 +12,7 @@
 DIRECTIONS = ((1, 0), (-1, 0), (0, 1), (0, -1), (1, 1), (1, -1), (-1, 1), (-1, -1))
 STARTS = (0, 16, 32, 48, 64, 72, 80, 88, 96)
 ROUNDS = 5
+LEVELS = (0, 1, -1)
 
 
 def derivative_table():
@@ -141,6 +142,14 @@
 
 def kernel(
     counts,
+    right_hbm,
+    geometry_hbm,
+    element_hbm,
+    vectors_hbm,
+    values_hbm,
+    select_hbm,
+    deep_hbm,
+    result_ref,
     right_ref,
     geometry_ref,
     element_ref,
@@ -148,7 +157,8 @@
     values_ref,
     select_ref,
     deep_ref,
-    result_ref,
+    start_send,
+    start_recv,
     right_recv,
     geometry_recv,
     class_recv,
@@ -168,6 +178,8 @@
     inverse_ref,
     sums_plane,
     sums_line,
+    load_sems,
+    start_sems,
     deep_sems,
     plane_sems,
     sum_send_sems,
@@ -180,6 +192,24 @@
     plane_size = nx * ny
     me_plane = gx * ny + gy
 
+    loads = [
+        pltpu.make_async_copy(source, target, load_sems.at[number])
+        for number, (source, target) in enumerate(
+            (
+                (right_hbm, right_ref),
+                (select_hbm, select_ref),
+                (element_hbm, element_ref),
+                (vectors_hbm, vectors_ref),
+                (values_hbm, values_ref),
+                (deep_hbm, deep_ref),
+                (geometry_hbm, geometry_ref),
+            )
+        )
+    ]
+    for load in loads:
+        load.start()
+
+    start_recv[...] = jnp.zeros_like(start_recv)
     right_recv[...] = jnp.zeros_like(right_recv)
     geometry_recv[...] = jnp.zeros_like(geometry_recv)
     class_recv[...] = jnp.zeros_like(class_recv)
@@ -194,7 +224,10 @@
         return other, (gx, gy, other)
 
     class_ref[...] = jnp.zeros_like(class_ref)
-    class_ref[0:1, 0:16] = element_ref[...].astype(F32)
+
+    def exists(dx, dy, dz):
+        x, y, z = gx + dx, gy + dy, gz + dz
+        return (x >= 0) & (x < nx) & (y >= 0) & (y < ny) & (z >= 0) & (z < nz)
 
     barrier = pltpu.get_barrier_semaphore()
     for offset in range(1, plane_size):
@@ -203,12 +236,24 @@
         )
     for offset in range(1, nz):
         pl.semaphore_signal(barrier, inc=1, device_id=line_partner(offset)[1], device_id_type=MESH)
-    pl.semaphore_wait(barrier, plane_size + nz - 2)
+    slanted = [(dx, dy, dz) for dz in (1, -1) for dx, dy in DIRECTIONS]
+    partners = plane_size + nz - 2
+    for step in slanted:
+        pl.when(exists(*step))(
+            lambda step=step: pl.semaphore_signal(
+                barrier,
+                inc=1,
+                device_id=(gx + step[0], gy + step[1], gz + step[2]),
+                device_id_type=MESH,
+            )
+        )
+        partners = partners + exists(*step).astype(jnp.int32)
+    pl.semaphore_wait(barrier, partners)
 
     inputs = (
-        (right_ref, right_recv),
+        (right_hbm, right_recv),
         (class_ref, class_recv),
-        (geometry_ref, geometry_recv),
+        (geometry_hbm, geometry_recv),
     )
 
     def deep_copy(number, step):
@@ -251,8 +296,26 @@
         )
 
     def plane_exists(dx, dy):
-        x, y = gx + dx, gy + dy
-        return (x >= 0) & (x < nx) & (y >= 0) & (y < ny)
+        return exists(dx, dy, 0)
+
+    def start_copy(level, at):
+        dx, dy = DIRECTIONS[at]
+        rows = pl.ds(STARTS[at], STARTS[at + 1] - STARTS[at])
+        return pltpu.make_async_remote_copy(
+            src_ref=start_send.at[rows],
+            dst_ref=start_recv.at[level, rows],
+            send_sem=start_sems.at[0, level, at],
+            recv_sem=start_sems.at[1, level, at],
+            device_id=(gx + dx, gy + dy, gz + LEVELS[level]),
+            device_id_type=MESH,
+        )
+
+    def start_each(action, sign):
+        for level, dz in enumerate(LEVELS):
+            for at, (dx, dy) in enumerate(DIRECTIONS):
+                pl.when(exists(sign * dx, sign * dy, sign * dz))(
+                    lambda level=level, at=at: action(start_copy(level, at))
+                )
 
     def plane_start(number, message):
         plane_send[number] = message
@@ -278,8 +341,8 @@
     def gather_plane_start(number, wide):
         plane_start(number, product(select_ref[0:96, 0:128], jnp.concatenate(halves(wide), 0)))
 
-    def gather_plane_end(number, wide):
-        both = jnp.concatenate([wide, plane_wait(number)], 0)
+    def gather_plane_end(wide, received):
+        both = jnp.concatenate([wide, received], 0)
         return pick(select_ref[96:256, 0:160], both)
 
     def scatter(number, extended):
@@ -330,10 +393,21 @@
 
     plane_weight = factor(rows // 8, 8, gx, nx) * factor(lax.rem(rows, 8), 8, gy, ny)
     weight = plane_weight * factor(lanes, 128, gz, nz)
+    deep_start(0)
+    loads[0].wait()
+    loads[1].wait()
     right = right_ref[...]
     weighted = weight * right
-    for number in range(3):
-        deep_start(number)
+    start_send[...] = product(
+        select_ref[0:96, 0:128], jnp.concatenate(halves(plane_weight * right), 0)
+    )
+    start_each(lambda copy: copy.start(), 1)
+    loads[2].wait()
+    class_ref[0:1, 0:16] = element_ref[...].astype(F32)
+    deep_start(1)
+    deep_start(2)
+    for load in loads[3:]:
+        load.wait()
 
     blank = jnp.zeros((6, 32), F32)
     groups = (
@@ -349,9 +423,6 @@
     high, low = halves(jnp.where(corner == along, jnp.concatenate([deep_ref[...]] * 32, 0), 0.0))
     deep_high[...] = high
     deep_low[...] = low
-    deep_wait(0)
-    wide = jnp.concatenate([plane_weight, plane_weight], 1) * widen(right, right_recv[...])
-    gather_plane_start(0, wide)
     deep_wait(1)
 
     def element_of(shape):
@@ -407,14 +478,19 @@
     third_high[...], third_low[...] = halves(spread)
     back_high[...], back_low[...] = halves(spread_back)
 
-    extended = gather_plane_end(0, wide)
+    deep_wait(0)
+    start_each(lambda copy: copy.wait_recv(), -1)
+    wide = jnp.concatenate([plane_weight, plane_weight], 1) * widen(right, right_recv[...])
+    extended = gather_plane_end(
+        wide, widen(start_recv[0], (start_recv[1], start_recv[2]))
+    )
     wide_precond = scatter(1, solve(extended))
     deep_wait(2)
     wide_geometry[...] = widen(geometry_ref[...], geometry_recv[...])
     image_local = local(wide_precond, *slopes_of(wide_precond))
     wide = sum_deep(image_local)
     gather_plane_start(2, wide)
-    extended = gather_plane_end(2, wide)
+    extended = gather_plane_end(wide, plane_wait(2))
     image = jnp.concatenate(
         [extended[16 * x + 1 : 16 * x + 9, 0:128] for x in range(1, 9)], 0
     )
@@ -468,7 +544,7 @@
         sum_copy(
             sums_line, line_send_sems, sum_line_sems, offset, gz, line_partner(offset)[1]
         ).start()
-    extended = gather_plane_end(4, wide)
+    extended = gather_plane_end(wide, plane_wait(4))
     again_image = jnp.concatenate(
         [extended[16 * x + 1 : 16 * x + 9, 0:128] for x in range(1, 9)], 0
     )
@@ -491,7 +567,8 @@
             pl.when(deep_exists(step))(
                 lambda number=number, step=step: deep_copy(number, step).wait_send()
             )
-    for number in range(ROUNDS):
+    start_each(lambda copy: copy.wait_send(), 1)
+    for number in range(1, ROUNDS):
         for at, (dx, dy) in enumerate(DIRECTIONS):
             pl.when(plane_exists(dx, dy))(
                 lambda number=number, at=at: plane_copy(number, at).wait_send()
@@ -513,9 +590,18 @@
     result = pl.pallas_call(
         lambda *refs: kernel(counts, *refs),
         out_shape=jax.ShapeDtypeStruct((2, 64, 128), F32),
-        in_specs=[vmem] * 7,
+        in_specs=[pl.BlockSpec(memory_space=pl.ANY)] * 7,
         out_specs=vmem,
         scratch_shapes=[
+            pltpu.VMEM((64, 128), F32),
+            pltpu.VMEM((256, 128), F32),
+            pltpu.VMEM((1, 16), jnp.int32),
+            pltpu.VMEM((10, 10, 3, 32), F32),
+            pltpu.VMEM((10, 3, 32), F32),
+            pltpu.VMEM((608, 256), BF16),
+            pltpu.VMEM((8, 256), F32),
+            pltpu.VMEM((96, 128), F32),
+            pltpu.VMEM((3, 96, 128), F32),
             pltpu.VMEM((2, 64, 128), F32),
             pltpu.VMEM((2, 256, 128), F32),
             pltpu.VMEM((2, 8, 128), F32),
@@ -535,6 +621,8 @@
             pltpu.VMEM((10, 16, 256), F32),
             pltpu.VMEM((nx * ny, 8, 128), F32),
             pltpu.VMEM((nz, 8, 128), F32),
+            pltpu.SemaphoreType.DMA((7,)),
+            pltpu.SemaphoreType.DMA((2, 3, 8)),
             pltpu.SemaphoreType.DMA((2, 3, 2)),
             pltpu.SemaphoreType.DMA((2, ROUNDS, 8)),
             pltpu.SemaphoreType.DMA((nx * ny,)),
@@ -543,7 +631,7 @@
             pltpu.SemaphoreType.DMA((nz,)),
         ],
         compiler_params=pltpu.CompilerParams(
-            collective_id=0, has_side_effects=True, vmem_limit_bytes=32 * 1024 * 1024
+            collective_id=0, has_side_effects=True, vmem_limit_bytes=60 * 1024 * 1024
         ),
     )(
         right_side.reshape(64, 128),

time: 38.8 us -> 35.5 us (0.915)
  local copies, waits for them, and re-layouts: 5.6 us -> 1.4 us
  Pallas kernels: 32.1 us -> 33.2 us
    unnamed x14 -> x0, local copies, waits for them, and re-layouts: 4.97 us -> none
    pallas_call x1, Pallas kernels: 32.1 us -> 33.2 us  [on_device(): pl.pallas_call(lambda *refs: kernel(counts, *refs), out_shape=jax.ShapeDt...]
    another operation x1, local copies, waits for them, and re-layouts: 0.63 us -> 1.4 us  [on_device(): return (result[0].reshape(shape), result[1].reshape(shape))]
where the time goes in v3:
time: 35.5 us; the launch traced here: 35.3 us
  Pallas kernels  33.2 us (94%)
  local copies, waits for them, and re-layouts  1.4 us (4%)
  between operations  0.64 us (2%)
    pallas_call x1, Pallas kernels, on_device(): pl.pallas_call(lambda *refs: kernel(counts, *refs), out_shape=jax.ShapeDt...  33.2 us
    another operation x1, local copies, waits for them, and re-layouts, on_device(): return (result[0].reshape(shape), result[1].reshape(shape))  1.4 us

profile of v3, /device:TPU:0, one launch (start us, length us, event | category | flops | bytes accessed | tf_op | source)
XLA Modules:
  0.0 35.3 jit_solution(1230935259751165859)
XLA Ops:
  0.6 33.2 %shard_map.86 = f32[2,64,128]{2,1,0:T(8,128)} custom-call(f32[64,128]{1,0:T(8,128)} %bitcast.11, f32[256,128]{1,0:T(8,128)} %bitcast.10, s32[1,16]{1,0:T(1,128)} %bitcast.13, f32[10,10,3,32]{3,2,1,0:T(4,128)} %bitcast.9, f32[10,3,32]{2,1,0:T(4,128)} %bitcast.12, bf16[608,256]{1,0:T(8,128)(2,1)} %constant.4.clone.refs_5_, f32[8,256]{1,0:T(8,128)} %constant.5.clone.refs_6_), custom_call_target="tpu_custom_call" | custom-call | tf_op jit(solution)/shard_map/pallas_call | solution.py:590
  33.9 1.4 %slice_bitcast_fusion = (f32[8,8,128]{2,1,0:T(8,128)}, f32[8,8,128]{2,1,0:T(8,128)}) fusion(f32[2,64,128]{2,1,0:T(8,128)} %shard_map.86), kind=kLoop, calls=%fused_computation | loop fusion | bytes 131072 | tf_op jit(solution)/shard_map/reshape;squeeze | solution.py:645

commit v4 on v3

--- a/solution.py
+++ b/solution.py
@@ -101,14 +101,6 @@
     return table
 
 
-def pieces(value):
-    high = value.astype(BF16)
-    rest = value - high.astype(F32)
-    middle = rest.astype(BF16)
-    low = (rest - middle.astype(F32)).astype(BF16)
-    return low, middle, high
-
-
 def halves(value):
     high = value.astype(BF16)
     return high, (value - high.astype(F32)).astype(BF16)
@@ -164,6 +156,9 @@
     class_recv,
     wide_geometry,
     class_ref,
+    entries_ref,
+    own_ref,
+    beside_ref,
     deep_high,
     deep_low,
     plane_send,
@@ -352,10 +347,11 @@
 
     def solve(extended):
         value = times(extended, third_high, third_low).reshape(10, 16, 256)
-        total = first_ref[0] * value[0][None]
+        value = value.reshape(10, 1, 2, 8, 256)
+        total = first_ref[0][:, None] * value[0]
         for a in range(1, 10):
-            total = total + first_ref[a] * value[a][None]
-        value = total
+            total = total + first_ref[a][:, None] * value[a]
+        value = total.reshape(10, 16, 256)
         total = second_ref[0][None] * value[:, 0:1, :]
         for b in range(1, 10):
             total = total + second_ref[b][None] * value[:, b : b + 1, :]
@@ -363,10 +359,10 @@
         total = second_back_ref[0][None] * value[:, 0:1, :]
         for n in range(1, 10):
             total = total + second_back_ref[n][None] * value[:, n : n + 1, :]
-        value = total
-        total = first_ref[:, 0] * value[0][None]
+        value = total.reshape(10, 1, 2, 8, 256)
+        total = first_ref[:, 0][:, None] * value[0]
         for m in range(1, 10):
-            total = total + first_ref[:, m] * value[m][None]
+            total = total + first_ref[:, m][:, None] * value[m]
         return times(total.reshape(160, 256), back_high, back_low, rows_rows)
 
     def slopes_of(field):
@@ -418,16 +414,30 @@
         + [values_ref[:, d, :] for d in (1, 0, 2)]
     )
     entries = jnp.concatenate([part for group in groups for part in (group, blank)], 0)
+    entries_ref[...] = jnp.concatenate(halves(entries), 1)
     corner = lax.broadcasted_iota(jnp.int32, (256, 256), 0) // 8
     along = lax.broadcasted_iota(jnp.int32, (256, 256), 1) // 8
     high, low = halves(jnp.where(corner == along, jnp.concatenate([deep_ref[...]] * 32, 0), 0.0))
     deep_high[...] = high
     deep_low[...] = low
-    deep_wait(1)
-
     def element_of(shape):
         place_at = lax.rem(lax.broadcasted_iota(jnp.int32, shape, 1), 24)
         return jnp.where(place_at < 20, place_at, place_at - 24)
+
+    node = lax.broadcasted_iota(jnp.int32, (256, 256), 0)
+    node = jnp.where(node < 192, node, node - 256)
+    element = element_of((256, 256))
+    reach = node - 8 * element
+    inside = (
+        (16 * gz + element >= 0)
+        & (16 * gz + element < 16 * nz)
+        & (128 * gz + node >= 0)
+        & (128 * gz + node < 128 * nz)
+    )
+    beside = (reach == -2) | (reach == -1) | (reach == 8) | (reach == 9)
+    own_ref[...] = jnp.where(inside & (reach >= 0) & (reach < 8), 1.0, 0.0)
+    beside_ref[...] = jnp.where(inside & beside, 1.0, 0.0)
+    deep_wait(1)
 
     source = lax.broadcasted_iota(jnp.int32, (384, 256), 0)
     source = jnp.where(source < 128, source, jnp.where(source < 256, source - 112, source - 272))
@@ -437,12 +447,12 @@
         (source == element_of((384, 256))).astype(F32).astype(BF16),
         preferred_element_type=F32,
     )[0:1]
-    kind = lax.broadcasted_iota(jnp.int32, (32, 256), 0).astype(F32)
+    kind = lax.rem(lax.broadcasted_iota(jnp.int32, (64, 256), 0), 32).astype(F32)
     chooser = (jnp.abs(kind - classes) < 0.5).astype(F32).astype(BF16)
-    table = place(entries, chooser, plain)
+    table = product(entries_ref[...], chooser)
     for a in range(10):
         for m in range(10):
-            first_ref[a, m] = jnp.broadcast_to(table[a * 16 + m : a * 16 + m + 1], (16, 256))
+            first_ref[a, m] = jnp.broadcast_to(table[a * 16 + m : a * 16 + m + 1], (8, 256))
     second_ref[...] = table[160:320].reshape(10, 16, 256)
     second_back_ref[...] = table[320:480].reshape(10, 16, 256)
     mode = lax.broadcasted_iota(jnp.int32, (1, 256), 1) // 24
@@ -454,29 +464,21 @@
 
     for m in range(10):
         inverse_ref[m] = 1.0 / (table[656 + m : 657 + m] + table[640:656] + level)
-    node = lax.broadcasted_iota(jnp.int32, (256, 256), 0)
-    node = jnp.where(node < 192, node, node - 256)
-    element = element_of((256, 256))
-    reach = node - 8 * element
-    slot = jnp.where(
-        reach == -2, 0, jnp.where(reach == 9, 9, jnp.where((reach >= 0) & (reach < 8), reach + 1, -1))
-    )
-    slot_back = jnp.where(reach == 8, 8, jnp.where(reach == -1, 1, slot))
-    inside = (
-        (16 * gz + element >= 0)
-        & (16 * gz + element < 16 * nz)
-        & (128 * gz + node >= 0)
-        & (128 * gz + node < 128 * nz)
-    )
-    slot = jnp.where(inside, slot, -1)
-    slot_back = jnp.where(inside, slot_back, -1)
-    spread = jnp.zeros((256, 256), F32)
-    spread_back = jnp.zeros((256, 256), F32)
-    for c in range(10):
-        spread = jnp.where(slot == c, third[c : c + 1], spread)
-        spread_back = jnp.where(slot_back == c, third[c : c + 1], spread_back)
-    third_high[...], third_low[...] = halves(spread)
-    back_high[...], back_low[...] = halves(spread_back)
+    ends = [third[c : c + 1] for c in (8, 9, 0, 1)]
+    none = jnp.zeros((4, 256), F32)
+    inner = third[1:9]
+    reached = jnp.concatenate([none[0:1], ends[1], none, ends[2], none[0:1]], 0)
+    shared = jnp.concatenate([ends[0], ends[1], none, ends[2], ends[3]], 0)
+    for outer, high_ref, low_ref in (
+        (reached, third_high, third_low),
+        (shared, back_high, back_low),
+    ):
+        for group in range(16):
+            at = pl.ds(16 * group, 16)
+            spread = own_ref[at] * jnp.concatenate([inner] * 2, 0) + beside_ref[
+                at
+            ] * jnp.concatenate([outer] * 2, 0)
+            high_ref[at], low_ref[at] = halves(spread)
 
     deep_wait(0)
     start_each(lambda copy: copy.wait_recv(), -1)
@@ -607,11 +609,14 @@
             pltpu.VMEM((2, 8, 128), F32),
             pltpu.VMEM((256, 256), F32),
             pltpu.VMEM((8, 128), F32),
+            pltpu.VMEM((688, 64), BF16),
+            pltpu.VMEM((256, 256), F32),
+            pltpu.VMEM((256, 256), F32),
             pltpu.VMEM((256, 256), BF16),
             pltpu.VMEM((256, 256), BF16),
             pltpu.VMEM((ROUNDS, 96, 256), F32),
             pltpu.VMEM((ROUNDS, 96, 256), F32),
-            pltpu.VMEM((10, 10, 16, 256), F32),
+            pltpu.VMEM((10, 10, 8, 256), F32),
             pltpu.VMEM((10, 16, 256), F32),
             pltpu.VMEM((10, 16, 256), F32),
             pltpu.VMEM((256, 256), BF16),

time: 35.5 us -> 34.5 us (0.972)
  Pallas kernels: 33.2 us -> 32.3 us
    pallas_call x1, Pallas kernels: 33.2 us -> 32.3 us  [on_device(): pl.pallas_call(lambda *refs: kernel(counts, *refs), out_shape=jax.ShapeDt...]
where the time goes in v4:
time: 34.5 us; the launch traced here: 34.4 us
  Pallas kernels  32.3 us (94%)
  local copies, waits for them, and re-layouts  1.4 us (4%)
  between operations  0.64 us (2%)
    pallas_call x1, Pallas kernels, on_device(): pl.pallas_call(lambda *refs: kernel(counts, *refs), out_shape=jax.ShapeDt...  32.3 us
    another operation x1, local copies, waits for them, and re-layouts, on_device(): return (result[0].reshape(shape), result[1].reshape(shape))  1.4 us

profile of v4, /device:TPU:0, one launch (start us, length us, event | category | flops | bytes accessed | tf_op | source)
XLA Modules:
  0.0 34.4 jit_solution(18120833470018445516)
XLA Ops:
  0.6 32.3 %shard_map.86 = f32[2,64,128]{2,1,0:T(8,128)} custom-call(f32[64,128]{1,0:T(8,128)} %bitcast.11, f32[256,128]{1,0:T(8,128)} %bitcast.10, s32[1,16]{1,0:T(1,128)} %bitcast.13, f32[10,10,3,32]{3,2,1,0:T(4,128)} %bitcast.9, f32[10,3,32]{2,1,0:T(4,128)} %bitcast.12, bf16[608,256]{1,0:T(8,128)(2,1)} %constant.4.clone.refs_5_, f32[8,256]{1,0:T(8,128)} %constant.5.clone.refs_6_), custom_call_target="tpu_custom_call" | custom-call | tf_op jit(solution)/shard_map/pallas_call | solution.py:592
  33.0 1.4 %slice_bitcast_fusion = (f32[8,8,128]{2,1,0:T(8,128)}, f32[8,8,128]{2,1,0:T(8,128)}) fusion(f32[2,64,128]{2,1,0:T(8,128)} %shard_map.86), kind=kLoop, calls=%fused_computation | loop fusion | bytes 131072 | tf_op jit(solution)/shard_map/reshape;squeeze | solution.py:650

commit v5 on v4

--- a/solution.py
+++ b/solution.py
@@ -46,7 +46,7 @@
     for place, (dx, dy) in enumerate(DIRECTIONS):
         xs = sent[dx] if dx else own
         ys = sent[dy] if dy else own
-        if dy and not dx:
+        if dy:
             pairs = [(x, y) for y in ys for x in xs]
         else:
             pairs = [(x, y) for x in xs for y in ys]
@@ -63,24 +63,16 @@
 
 
 def selections():
-    gather_from = {1: (7, 8), -1: (2, 1)}
-    gather_to = {1: (0, 1), -1: (9, 8)}
-    scatter_from = {1: (9, 8), -1: (0, 1)}
-    scatter_to = {1: (2, 1), -1: (7, 8)}
-    pack_gather = np.zeros((96, 128))
+    gather_to = {1: (0, 1), -1: (8, 9)}
+    scatter_to = {1: (1, 2), -1: (7, 8)}
     unpack_gather = np.zeros((160, 160))
-    pack_scatter = np.zeros((96, 160))
     unpack_scatter = np.zeros((64, 256))
     for x in range(1, 9):
         for y in range(1, 9):
             unpack_gather[slot_row(x, y), node_row(x, y)] = 1
             unpack_scatter[node_row(x, y), slot_row(x, y)] = 1
-    for row, x, y in message_rows(gather_from):
-        pack_gather[row, [node_row(x, y), 64 + node_row(x, y)]] = 1
     for row, x, y in message_rows(gather_to):
         unpack_gather[slot_row(x, y), 64 + row] = 1
-    for row, x, y in message_rows(scatter_from):
-        pack_scatter[row, slot_row(x, y)] = 1
     for row, x, y in message_rows(scatter_to):
         unpack_scatter[node_row(x, y), 160 + row] = 1
     derivative = derivative_table()
@@ -88,17 +80,44 @@
     plane = np.concatenate([np.kron(derivative, eye), np.kron(eye, derivative)], 0)
     high = np.asarray(np.asarray(plane, BF16), np.float64)
     low = plane - high
-    table = np.zeros((608, 256))
+    table = np.zeros((416, 256))
     for start, part in (
-        (0, pack_gather),
-        (96, unpack_gather),
-        (256, pack_scatter),
-        (352, unpack_scatter),
-        (416, np.concatenate([high, high, low], 1)),
-        (544, np.concatenate([high.T, low.T], 1)),
+        (0, unpack_gather),
+        (160, unpack_scatter),
+        (224, np.concatenate([high, high, low], 1)),
+        (352, np.concatenate([high.T, low.T], 1)),
     ):
         table[start : start + part.shape[0], : part.shape[1]] = part
     return table
+
+
+def message(faces, columns):
+    rows = list(faces)
+    for pair in columns:
+        rows += [nodes for _, nodes, _ in pair]
+    blank = jnp.zeros((4,) + rows[0].shape[1:], F32)
+    for side in (2, 0):
+        for pair in columns:
+            rows += [layer[side] for layer in pair] + [blank]
+    return jnp.concatenate(rows, 0)
+
+
+def gather_message(field):
+    cube = field.reshape(8, 8, field.shape[1])
+    columns = []
+    for pair in ((6, 7), (0, 1)):
+        layers = [cube[:, y, :] for y in pair]
+        columns.append([(layer[0:2], layer, layer[6:8]) for layer in layers])
+    return message((field[48:64], field[0:16]), columns)
+
+
+def scatter_message(extended):
+    cube = extended.reshape(10, 16, extended.shape[1])
+    columns = []
+    for pair in ((8, 9), (0, 1)):
+        layers = [cube[:, y, :] for y in pair]
+        columns.append([(layer[0:2], layer[1:9], layer[8:10]) for layer in layers])
+    return message([cube[x, 1:9] for x in (8, 9, 0, 1)], columns)
 
 
 def halves(value):
@@ -334,16 +353,16 @@
         return field + following + previous
 
     def gather_plane_start(number, wide):
-        plane_start(number, product(select_ref[0:96, 0:128], jnp.concatenate(halves(wide), 0)))
+        plane_start(number, gather_message(wide))
 
     def gather_plane_end(wide, received):
         both = jnp.concatenate([wide, received], 0)
-        return pick(select_ref[96:256, 0:160], both)
+        return pick(select_ref[0:160, 0:160], both)
 
     def scatter(number, extended):
-        plane_start(number, pick(select_ref[256:352, 0:160], extended))
+        plane_start(number, scatter_message(extended))
         both = jnp.concatenate([extended, plane_wait(number)], 0)
-        return pick(select_ref[352:416, :], both)
+        return pick(select_ref[160:224, :], both)
 
     def solve(extended):
         value = times(extended, third_high, third_low).reshape(10, 16, 256)
@@ -367,15 +386,15 @@
 
     def slopes_of(field):
         high, low = halves(field)
-        slopes = product(select_ref[416:544, 0:192], jnp.concatenate([high, low, high], 0))
+        slopes = product(select_ref[224:352, 0:192], jnp.concatenate([high, low, high], 0))
         return slopes, times(field, deep_high, deep_low)
 
     def local(field, slopes, deep):
         high, low = halves(wide_geometry[0:128] * slopes)
         back = (
-            product(select_ref[544:608, 0:128], low)
-            + product(select_ref[544:608, 128:256], high)
-            + product(select_ref[544:608, 0:128], high)
+            product(select_ref[352:416, 0:128], low)
+            + product(select_ref[352:416, 128:256], high)
+            + product(select_ref[352:416, 0:128], high)
         )
         deep = times(wide_geometry[128:192] * deep, deep_high, deep_low, rows_rows)
         return back + deep + wide_geometry[192:256] * field
@@ -391,18 +410,15 @@
     weight = plane_weight * factor(lanes, 128, gz, nz)
     deep_start(0)
     loads[0].wait()
-    loads[1].wait()
     right = right_ref[...]
     weighted = weight * right
-    start_send[...] = product(
-        select_ref[0:96, 0:128], jnp.concatenate(halves(plane_weight * right), 0)
-    )
+    start_send[...] = gather_message(plane_weight * right)
     start_each(lambda copy: copy.start(), 1)
     loads[2].wait()
     class_ref[0:1, 0:16] = element_ref[...].astype(F32)
     deep_start(1)
     deep_start(2)
-    for load in loads[3:]:
+    for load in loads[1:2] + loads[3:]:
         load.wait()
 
     blank = jnp.zeros((6, 32), F32)
@@ -550,20 +566,6 @@
     again_image = jnp.concatenate(
         [extended[16 * x + 1 : 16 * x + 9, 0:128] for x in range(1, 9)], 0
     )
-    for offset in range(1, nz):
-        sum_wait(sums_line, sum_line_sems, line_partner(offset)[0])
-    sums = jnp.sum(jnp.sum(sums_line[...], 0), 1, keepdims=True)
-    a, b, c, d, f = [sums[k : k + 1] for k in range(5)]
-    step_one = a / b
-    rho = a - step_one * (b + c) + step_one * step_one * d
-    stretch = 1.0 + rho / a
-    curvature = stretch * stretch * b - 2.0 * stretch * step_one * d + step_one * step_one * f
-    step_two = rho / curvature
-    on_precond = step_one + step_two * stretch
-    on_again = step_one * step_two
-    result_ref[0] = on_precond * precond - on_again * again
-    result_ref[1] = right - on_precond * image + on_again * again_image
-
     for number in range(3):
         for step in (1, -1):
             pl.when(deep_exists(step))(
@@ -584,6 +586,20 @@
             sums_line, line_send_sems, sum_line_sems, offset, gz, line_partner(offset)[1]
         ).wait_send()
 
+    for offset in range(1, nz):
+        sum_wait(sums_line, sum_line_sems, line_partner(offset)[0])
+    sums = jnp.sum(jnp.sum(sums_line[...], 0), 1, keepdims=True)
+    a, b, c, d, f = [sums[k : k + 1] for k in range(5)]
+    step_one = a / b
+    rho = a - step_one * (b + c) + step_one * step_one * d
+    stretch = 1.0 + rho / a
+    curvature = stretch * stretch * b - 2.0 * stretch * step_one * d + step_one * step_one * f
+    step_two = rho / curvature
+    on_precond = step_one + step_two * stretch
+    on_again = step_one * step_two
+    result_ref[0] = on_precond * precond - on_again * again
+    result_ref[1] = right - on_precond * image + on_again * again_image
+
 
 def on_device(counts, right_side, geometry, element_shape_class, fdm_vectors, fdm_values):
     nx, ny, nz = counts
@@ -600,7 +616,7 @@
             pltpu.VMEM((1, 16), jnp.int32),
             pltpu.VMEM((10, 10, 3, 32), F32),
             pltpu.VMEM((10, 3, 32), F32),
-            pltpu.VMEM((608, 256), BF16),
+            pltpu.VMEM((416, 256), BF16),
             pltpu.VMEM((8, 256), F32),
             pltpu.VMEM((96, 128), F32),
             pltpu.VMEM((3, 96, 128), F32),

time: 34.5 us -> 34 us (0.986)
  Pallas kernels: 32.3 us -> 31.7 us
    pallas_call x1, Pallas kernels: 32.3 us -> 31.7 us  [on_device(): pl.pallas_call(lambda *refs: kernel(counts, *refs), out_shape=jax.ShapeDt...]
where the time goes in v5:
time: 34 us; the launch traced here: 33.8 us
  Pallas kernels  31.7 us (93%)
  local copies, waits for them, and re-layouts  1.4 us (4%)
  between operations  0.64 us (2%)
    pallas_call x1, Pallas kernels, on_device(): pl.pallas_call(lambda *refs: kernel(counts, *refs), out_shape=jax.ShapeDt...  31.7 us
    another operation x1, local copies, waits for them, and re-layouts, on_device(): return (result[0].reshape(shape), result[1].reshape(shape))  1.4 us

profile of v5, /device:TPU:0, one launch (start us, length us, event | category | flops | bytes accessed | tf_op | source)
XLA Modules:
  0.0 33.8 jit_solution(14534180009477327204)
XLA Ops:
  0.6 31.7 %shard_map.86 = f32[2,64,128]{2,1,0:T(8,128)} custom-call(f32[64,128]{1,0:T(8,128)} %bitcast.11, f32[256,128]{1,0:T(8,128)} %bitcast.10, s32[1,16]{1,0:T(1,128)} %bitcast.13, f32[10,10,3,32]{3,2,1,0:T(4,128)} %bitcast.9, f32[10,3,32]{2,1,0:T(4,128)} %bitcast.12, bf16[416,256]{1,0:T(8,128)(2,1)} %constant.4.clone.refs_5_, f32[8,256]{1,0:T(8,128)} %constant.5.clone.refs_6_), custom_call_target="tpu_custom_call" | custom-call | tf_op jit(solution)/shard_map/pallas_call | solution.py:608
  32.4 1.4 %slice_bitcast_fusion = (f32[8,8,128]{2,1,0:T(8,128)}, f32[8,8,128]{2,1,0:T(8,128)}) fusion(f32[2,64,128]{2,1,0:T(8,128)} %shard_map.86), kind=kLoop, calls=%fused_computation | loop fusion | bytes 131072 | tf_op jit(solution)/shard_map/reshape;squeeze | solution.py:666

commit v6 on v5

--- a/solution.py
+++ b/solution.py
@@ -174,6 +174,7 @@
     geometry_recv,
     class_recv,
     wide_geometry,
+    image_ref,
     class_ref,
     entries_ref,
     own_ref,
@@ -359,8 +360,9 @@
         both = jnp.concatenate([wide, received], 0)
         return pick(select_ref[0:160, 0:160], both)
 
-    def scatter(number, extended):
+    def scatter(number, extended, meanwhile):
         plane_start(number, scatter_message(extended))
+        meanwhile()
         both = jnp.concatenate([extended, plane_wait(number)], 0)
         return pick(select_ref[160:224, :], both)
 
@@ -502,17 +504,24 @@
     extended = gather_plane_end(
         wide, widen(start_recv[0], (start_recv[1], start_recv[2]))
     )
-    wide_precond = scatter(1, solve(extended))
-    deep_wait(2)
-    wide_geometry[...] = widen(geometry_ref[...], geometry_recv[...])
+
+    def load_geometry():
+        deep_wait(2)
+        wide_geometry[...] = widen(geometry_ref[...], geometry_recv[...])
+
+    wide_precond = scatter(1, solve(extended), load_geometry)
     image_local = local(wide_precond, *slopes_of(wide_precond))
     wide = sum_deep(image_local)
     gather_plane_start(2, wide)
     extended = gather_plane_end(wide, plane_wait(2))
-    image = jnp.concatenate(
-        [extended[16 * x + 1 : 16 * x + 9, 0:128] for x in range(1, 9)], 0
-    )
-    wide_again = scatter(3, solve(extended))
+
+    def keep_image():
+        image_ref[...] = jnp.concatenate(
+            [extended[16 * x + 1 : 16 * x + 9, 0:128] for x in range(1, 9)], 0
+        )
+
+    wide_again = scatter(3, solve(extended), keep_image)
+    image = image_ref[...]
     slopes, deep = slopes_of(wide_again)
     precond, again = wide_precond[:, 0:128], wide_again[:, 0:128]
 
@@ -624,6 +633,7 @@
             pltpu.VMEM((2, 256, 128), F32),
             pltpu.VMEM((2, 8, 128), F32),
             pltpu.VMEM((256, 256), F32),
+            pltpu.VMEM((64, 128), F32),
             pltpu.VMEM((8, 128), F32),
             pltpu.VMEM((688, 64), BF16),
             pltpu.VMEM((256, 256), F32),

time: 34 us -> 33.9 us (level)
  no operation moved by 1% of the time
where the time goes in v6:
time: 33.9 us; the launch traced here: 33.8 us
  Pallas kernels  31.7 us (94%)
  local copies, waits for them, and re-layouts  1.4 us (4%)
  between operations  0.64 us (2%)
    pallas_call x1, Pallas kernels, on_device(): pl.pallas_call(lambda *refs: kernel(counts, *refs), out_shape=jax.ShapeDt...  31.7 us
    another operation x1, local copies, waits for them, and re-layouts, on_device(): return (result[0].reshape(shape), result[1].reshape(shape))  1.4 us

profile of v6, /device:TPU:0, one launch (start us, length us, event | category | flops | bytes accessed | tf_op | source)
XLA Modules:
  0.0 33.8 jit_solution(7473095031947876085)
XLA Ops:
  0.6 31.7 %shard_map.86 = f32[2,64,128]{2,1,0:T(8,128)} custom-call(f32[64,128]{1,0:T(8,128)} %bitcast.11, f32[256,128]{1,0:T(8,128)} %bitcast.10, s32[1,16]{1,0:T(1,128)} %bitcast.13, f32[10,10,3,32]{3,2,1,0:T(4,128)} %bitcast.9, f32[10,3,32]{2,1,0:T(4,128)} %bitcast.12, bf16[416,256]{1,0:T(8,128)(2,1)} %constant.4.clone.refs_5_, f32[8,256]{1,0:T(8,128)} %constant.5.clone.refs_6_), custom_call_target="tpu_custom_call" | custom-call | tf_op jit(solution)/shard_map/pallas_call | solution.py:617
  32.4 1.4 %slice_bitcast_fusion = (f32[8,8,128]{2,1,0:T(8,128)}, f32[8,8,128]{2,1,0:T(8,128)}) fusion(f32[2,64,128]{2,1,0:T(8,128)} %shard_map.86), kind=kLoop, calls=%fused_computation | loop fusion | bytes 131072 | tf_op jit(solution)/shard_map/reshape;squeeze | solution.py:676
